TPU v7x, 1024 devices: a whole 4x8x16 slice. The times are simulated.
1024 devices in a mesh: grid: 256 (over z, y, x_hi), layer: 4 (over x_lo, core).
Axes of the slice: x: 4 (x_hi: 2, x_lo: 2; x = x_hi * 2 + x_lo), y: 8, z: 16, core: 2. Of those that a mesh axis runs over, the one named last changes fastest.
Arguments:
- x_panel: bfloat16 [65536, 256], P(('grid', 'layer')), may hold values from -6 to 6
- b_panel: bfloat16 [65536, 256], P(('grid', 'layer')), may hold values from -6 to 6
- a_blocks: bfloat16 [1024, 4, 64, 64, 64], P('grid', 'layer'), may hold values from -0.046875 to 0.046875
- a_inner: int32 [1024, 4, 64], P('grid', 'layer'), may hold values from 0 to 255, as said below
- a_count: int32 [1024, 4], P('grid', 'layer'), may hold values from 16 to 64, as said below
Outputs:
- new_panel: bfloat16 [65536, 256], P(('grid', 'layer'))
Inputs may be any that keep to these rules, and one draw needn't show every extreme that they name: `a_inner`: within each row cluster and layer the entries are distinct and ascending. `a_count`: some row cluster and layer has all 64 slots live in every draw.
All inputs are finite; a program needn't handle non-finite values.
Results may differ from a plain program's by a relative error of at most 0.001.
Values may be sent and summed in bfloat16 or wider, within the bound.
No kernel may reach another device: no remote copies, remote signals or barrier semaphores. Data moves between devices by JAX's collectives and lax.ppermute only.
A program may use at most 64 MiB of HBM per device.

v0:
```python
import jax
import jax.numpy as jnp
from jax import lax
from jax.sharding import PartitionSpec as P


def cluster_products(blocks, inner, live_mask, grouped, first):
    count_here = grouped.shape[0]
    position = inner - first
    usable = live_mask & (position >= 0) & (position < count_here)
    clipped = jnp.clip(position, 0, count_here - 1)

    def one_cluster(item):
        row_blocks, row_pos, row_use = item
        chosen = jnp.take(grouped, row_pos, axis=0)
        chosen = jnp.where(row_use[:, None, None], chosen, jnp.zeros_like(chosen))
        return jnp.einsum("sij,sjc->ic", row_blocks, chosen, preferred_element_type=jnp.float32)

    return lax.map(one_cluster, (blocks, clipped, usable))


def per_device(x_panel, b_panel, a_blocks, a_inner, a_count):
    row_count = a_blocks.shape[0]
    slot_count = a_blocks.shape[2]
    block_size = a_blocks.shape[3]
    columns = b_panel.shape[1]
    blocks = a_blocks[:, 0]
    inner = a_inner[:, 0, :]
    live_mask = jnp.arange(slot_count, dtype=jnp.int32)[None, :] < a_count
    gathered = lax.all_gather(b_panel, "grid", axis=0, tiled=True)
    grouped = gathered.reshape(-1, block_size, columns)
    partial_value = cluster_products(blocks, inner, live_mask, grouped, 0)
    flat = partial_value.reshape(row_count * block_size, columns)
    summed = lax.psum(flat, "layer")
    share = flat.shape[0] // lax.axis_size("layer")
    mine = lax.dynamic_slice_in_dim(summed, lax.axis_index("layer") * share, share, 0)
    return (1.5 * x_panel.astype(jnp.float32) - 0.5 * mine).astype(jnp.bfloat16)


def solution(mesh):
    placed = (
        P(("grid", "layer"), None),
        P(("grid", "layer"), None),
        P("grid", "layer", None, None, None),
        P("grid", "layer", None),
        P("grid", "layer"),
    )
    return jax.shard_map(
        per_device,
        mesh=mesh,
        in_specs=placed,
        out_specs=P(("grid", "layer"), None),
        check_vma=False,
    )
```

profile of v0, /device:TPU:1, one launch (start us, length us, event | category | flops | bytes accessed | tf_op | source)
XLA Modules:
  0.0 372.9 jit_solution(13814374013706311081)
XLA Ops:
  6.5 0.0 all-gather.2.cloned.1.call-start
  6.5 0.7 all-gather.2.cloned.1.call-update
  7.3 0.0 all-reduce.2.cloned.1.call-start
  7.3 0.0 copy-start.1
  7.3 0.0 copy-start.2
  7.3 7.5 %copy.7 = bf16[4,1,64,64,64]{2,3,4,0,1:T(8,128)(2,1)} copy(bf16[4,1,64,64,64]{4,3,2,1,0:T(8,128)(2,1)} %param.9) | data formatting | bytes 4194304 | tf_op args[2]
  14.8 0.0 copy-done.1
  14.8 0.0 copy-done.2
  14.8 0.1 fusion.13
  14.9 252.8 %all-gather.2.cloned.1.call-done = bf16[16384,256]{1,0:T(8,128)(2,1)} async-done(((bf16[64,256]{1,0:T(8,128)(2,1)}), bf16[16384,256]{1,0:T(8,128)(2,1)}) %all-gather.2.cloned.1.call-update) | async-done | bytes 8388624 | tf_op jit(solution)/shard_map/all_gather | solution.py:30
  267.7 0.0 copy-start
  267.7 35.0 %while.10 = (s32[]{:T(128)}, f32[4,64,256]{2,1,0:T(8,128)}, bf16[4,64,64,64]{1,2,3,0:T(8,128)(2,1)}, pred[4,64]{1,0:T(4,128)(4,1)S(1)}, s32[4,64]{1,0:T(4,128)S(1)}, /*index=5*/bf16[256,64,256]{2,1,0:T(8,128)(2,1)}, s32[]{:T(128)}) while((s32[]{:T(128)}, f32[4,64,256]{2,1,0:T(8,128)}, bf16[4,64,64,64]{1,2,3,0:T(8,128)(2,1)}, ...), condition=%wide.region_1.2_spmd, body=%wide.region_0.1_spmd.sunk | while | flops 136316480 | bytes 11606681 | solution.py:19
  267.7 4.1 %gather_fusion = bf16[64,64,256]{2,1,0:T(8,128)(2,1)S(1)} fusion(bf16[256,64,256]{2,1,0:T(8,128)(2,1)} %get-tuple-element.106, s32[1024]{0:T(1024)S(1)} %pad_clamp_fusion.2), kind=kCustom, calls=%fused_computation.clone.1 | custom fusion | bytes 4194560 | tf_op jit(solution)/shard_map/while/body/eval_jaxpr/jit(_take)/gather | solution.py:15
  271.8 0.3 select_select_fusion.2
  272.2 4.3 %fusion.21 = f32[4,64,256]{2,1,0:T(8,128)} fusion(f32[4,64,256]{2,1,0:T(8,128)} %get-tuple-element.95, s32[]{:T(128)} %get-tuple-element.94, bf16[64,64,256]{2,1,0:T(8,128)(2,1)S(1)} %select_select_fusion.2, bf16[4,64,64,64]{1,2,3,0:T(8,128)(2,1)} %get-tuple-element.103), kind=kOutput, calls=%fused_computation.5.clone.1 | convolution fusion | flops 134217728 | bytes 3212288 | tf_op jit(solution)/shard_map/while/body/eval_jaxpr/sij,sjc->ic/dot_general | solution.py:17
  276.5 4.1 %gather_fusion = bf16[64,64,256]{2,1,0:T(8,128)(2,1)S(1)} fusion(bf16[256,64,256]{2,1,0:T(8,128)(2,1)} %get-tuple-element.106, s32[1024]{0:T(1024)S(1)} %pad_clamp_fusion.2), kind=kCustom, calls=%fused_computation.clone.1 | custom fusion | bytes 4194560 | tf_op jit(solution)/shard_map/while/body/eval_jaxpr/jit(_take)/gather | solution.py:15
  280.6 0.3 select_select_fusion.2
  280.9 4.3 %fusion.21 = f32[4,64,256]{2,1,0:T(8,128)} fusion(f32[4,64,256]{2,1,0:T(8,128)} %get-tuple-element.95, s32[]{:T(128)} %get-tuple-element.94, bf16[64,64,256]{2,1,0:T(8,128)(2,1)S(1)} %select_select_fusion.2, bf16[4,64,64,64]{1,2,3,0:T(8,128)(2,1)} %get-tuple-element.103), kind=kOutput, calls=%fused_computation.5.clone.1 | convolution fusion | flops 134217728 | bytes 3212288 | tf_op jit(solution)/shard_map/while/body/eval_jaxpr/sij,sjc->ic/dot_general | solution.py:17
  285.2 4.1 %gather_fusion = bf16[64,64,256]{2,1,0:T(8,128)(2,1)S(1)} fusion(bf16[256,64,256]{2,1,0:T(8,128)(2,1)} %get-tuple-element.106, s32[1024]{0:T(1024)S(1)} %pad_clamp_fusion.2), kind=kCustom, calls=%fused_computation.clone.1 | custom fusion | bytes 4194560 | tf_op jit(solution)/shard_map/while/body/eval_jaxpr/jit(_take)/gather | solution.py:15
  289.3 0.3 select_select_fusion.2
  289.7 4.3 %fusion.21 = f32[4,64,256]{2,1,0:T(8,128)} fusion(f32[4,64,256]{2,1,0:T(8,128)} %get-tuple-element.95, s32[]{:T(128)} %get-tuple-element.94, bf16[64,64,256]{2,1,0:T(8,128)(2,1)S(1)} %select_select_fusion.2, bf16[4,64,64,64]{1,2,3,0:T(8,128)(2,1)} %get-tuple-element.103), kind=kOutput, calls=%fused_computation.5.clone.1 | convolution fusion | flops 134217728 | bytes 3212288 | tf_op jit(solution)/shard_map/while/body/eval_jaxpr/sij,sjc->ic/dot_general | solution.py:17
  294.0 4.1 %gather_fusion = bf16[64,64,256]{2,1,0:T(8,128)(2,1)S(1)} fusion(bf16[256,64,256]{2,1,0:T(8,128)(2,1)} %get-tuple-element.106, s32[1024]{0:T(1024)S(1)} %pad_clamp_fusion.2), kind=kCustom, calls=%fused_computation.clone.1 | custom fusion | bytes 4194560 | tf_op jit(solution)/shard_map/while/body/eval_jaxpr/jit(_take)/gather | solution.py:15
  298.1 0.3 select_select_fusion.2
  298.4 4.3 %fusion.21 = f32[4,64,256]{2,1,0:T(8,128)} fusion(f32[4,64,256]{2,1,0:T(8,128)} %get-tuple-element.95, s32[]{:T(128)} %get-tuple-element.94, bf16[64,64,256]{2,1,0:T(8,128)(2,1)S(1)} %select_select_fusion.2, bf16[4,64,64,64]{1,2,3,0:T(8,128)(2,1)} %get-tuple-element.103), kind=kOutput, calls=%fused_computation.5.clone.1 | convolution fusion | flops 134217728 | bytes 3212288 | tf_op jit(solution)/shard_map/while/body/eval_jaxpr/sij,sjc->ic/dot_general | solution.py:17
  302.7 0.0 all-reduce.2.cloned.1.call-update
  302.7 61.8 %all-reduce.2.cloned.1.call-done = f32[256,256]{1,0:T(8,128)} async-done(((f32[256,256]{1,0:T(8,128)}), f32[256,256]{1,0:T(8,128)}) %all-reduce.2.cloned.1.call-update) | async-done | bytes 262160 | tf_op jit(solution)/shard_map/psum | solution.py:34
  364.6 0.0 copy-done
  364.6 1.5 subtract_convert_fusion
  (18 shorter events, 0.2 us)
Async XLA Ops:
  6.5 261.2 %all-gather.2.cloned.1.call-start = ((), (), s32[]{:S(2)}) async-start(), calls=%async_computation | async-start | bytes 8421376 | tf_op jit(solution)/shard_map/all_gather | solution.py:30
  7.3 357.3 %all-reduce.2.cloned.1.call-start = ((), (), s32[]{:S(2)}) async-start(), calls=%async_computation.1 | async-start | bytes 524288 | tf_op jit(solution)/shard_map/psum | solution.py:34
  7.3 7.5 %copy-start.1 = (s32[4,1,64]{2,1,0:T(1,128)S(1)}, s32[4,1,64]{2,1,0:T(1,128)}, u32[]{:S(2)}) copy-start(s32[4,1,64]{2,1,0:T(1,128)} %param.10) | copy-start | bytes 3076
  7.3 7.5 %copy-start.2 = (s32[4,1]{0,1:T(1,128)S(1)}, s32[4,1]{0,1:T(1,128)}, u32[]{:S(2)}) copy-start(s32[4,1]{0,1:T(1,128)} %param.11) | copy-start | bytes 52
  267.7 96.9 %copy-start = (bf16[64,256]{1,0:T(8,128)(2,1)S(1)}, bf16[64,256]{1,0:T(8,128)(2,1)}, u32[]{:S(2)}) copy-start(bf16[64,256]{1,0:T(8,128)(2,1)} %param.7) | copy-start | bytes 98308
Sparse Core Ops, SparseCore 0:
  13.2 254.5 all-gather.1
  302.9 61.6 all-reduce.1
where the time goes:
time: 373 us
  waiting for transfers between devices  315 us (84%)
  local copies, waits for them, and re-layouts  23.8 us (6%)
  matrix products  17.2 us (5%)
  between operations  13.4 us (4%)
    all_gather x1, waiting for transfers between devices, per_device(): gathered = lax.all_gather(b_panel, 'grid', axis=0, tiled=True)  253 us
    psum x1, waiting for transfers between devices, per_device(): summed = lax.psum(flat, 'layer')  61.8 us
    dot_general x4, matrix products, one_cluster(): jnp.einsum('sij,sjc->ic', row_blocks, chosen, preferred_element_type=jnp....  17.2 us
    gather x4, local copies, waits for them, and re-layouts, one_cluster(): chosen = jnp.take(grouped, row_pos, axis=0)  16.2 us
    unnamed x7, local copies, waits for them, and re-layouts  7.47 us
  transfers between devices with their start and end apart: 2, of which 2 were waited for; matrix products, arithmetic and copies ran while one was open for 2% of the time, Pallas kernels for 0%

commit v1 on v0

v1 whole, which is shorter than its diff:
```python
import functools

import jax
import jax.numpy as jnp
import numpy as np
from jax import lax
from jax.experimental import pallas as pl
from jax.experimental.pallas import tpu as pltpu
from jax.sharding import Mesh
from jax.sharding import PartitionSpec as P

NEAR = 4
NZF, NYF, NXH, NXL, NC = 4, 2, 2, 2, 2
NZ, NY = NZF * NEAR, NYF * NEAR
Z, Y = ("zf", "zn"), ("yf", "yn")
AXES = Z + Y + ("xh", "xl", "c")
DIMS = (NZF, NEAR, NYF, NEAR, NXH, NXL, NC)
BS = 64
HALF = 128
WIDE = 256
PER_TILE = WIDE // BS
CLUSTERS = 256
TILES = CLUSTERS // PER_TILE
STEP_TILES = 8
MIB = 1024 * 1024


def pack_kernel(index_ref, a_ref, out_ref):
    pairs = a_ref.shape[2] // 2
    for pair in range(pairs):
        out_ref[0, pair] = jnp.concatenate([a_ref[0, 0, 2 * pair], a_ref[0, 0, 2 * pair + 1]], axis=-1)
    index = index_ref[0].astype(jnp.float32)
    out_ref[0, pairs] = jnp.broadcast_to(jnp.concatenate([index, index], axis=-1), (BS, 2 * BS)).astype(out_ref.dtype)


def pack(a_blocks, masked):
    rows, _, slots, bs, _ = a_blocks.shape
    return pl.pallas_call(
        pack_kernel,
        grid=(rows,),
        in_specs=[
            pl.BlockSpec((1, 1, slots), lambda r: (r, 0, 0)),
            pl.BlockSpec((1, 1, slots, bs, bs), lambda r: (r, 0, 0, 0, 0)),
        ],
        out_specs=pl.BlockSpec((1, slots // 2 + 1, bs, 2 * bs), lambda r: (r, 0, 0, 0)),
        out_shape=jax.ShapeDtypeStruct((rows, slots // 2 + 1, bs, 2 * bs), a_blocks.dtype),
        cost_estimate=pl.CostEstimate(flops=0, bytes_accessed=6 * MIB, transcendentals=0),
        compiler_params=pltpu.CompilerParams(vmem_limit_bytes=8 * MIB),
    )(masked, a_blocks)


def spread_kernel(pos_ref, packed_ref, out_ref):
    row = pl.program_id(0)
    lane = lax.broadcasted_iota(jnp.int32, (BS, 2 * BS), 1)
    out_ref[...] = jnp.zeros_like(out_ref)

    def one_pair(pair, carry):
        straight = packed_ref[0, pair]
        swapped = jnp.concatenate([straight[:, BS:], straight[:, :BS]], axis=-1)
        for side in range(2):
            pos = pos_ref[row, 2 * pair + side]
            tile = pos // PER_TILE
            within = pos % PER_TILE
            at = pl.ds(pl.multiple_of((within // 2) * (2 * BS), 2 * BS), 2 * BS)
            to_side = within % 2
            value = jnp.where(to_side == side, straight, swapped)
            mine = (lane >= BS) == (to_side == 1)
            out_ref[tile, :, at] = jnp.where(mine, value, out_ref[tile, :, at])
        return carry

    lax.fori_loop(0, packed_ref.shape[1], one_pair, 0, unroll=4)


def spread(packed, pos):
    rows, more, bs, wide = packed.shape
    return pl.pallas_call(
        spread_kernel,
        grid_spec=pltpu.PrefetchScalarGridSpec(
            num_scalar_prefetch=1,
            grid=(rows,),
            in_specs=[pl.BlockSpec((1, more - 1, bs, wide), lambda r, pos: (r, 0, 0, 0))],
            out_specs=pl.BlockSpec((TILES + 1, bs, WIDE), lambda r, pos: (0, r, 0)),
        ),
        out_shape=jax.ShapeDtypeStruct((TILES + 1, rows * bs, WIDE), packed.dtype),
        cost_estimate=pl.CostEstimate(flops=0, bytes_accessed=20 * MIB, transcendentals=0),
        compiler_params=pltpu.CompilerParams(vmem_limit_bytes=8 * MIB),
    )(pos, packed)


def multiply_kernel(has_acc, own_ref, other_ref, b_ref, *rest):
    out_ref = rest[-1]
    rows = own_ref.shape[1]

    @pl.when(pl.program_id(0) == 0)
    def _():
        out_ref[...] = rest[0][...] if has_acc else jnp.zeros_like(out_ref)

    for half, ref in enumerate((own_ref, other_ref)):
        total = out_ref[half]
        for t in range(ref.shape[0]):
            total = total + jnp.dot(ref[t], b_ref[t * WIDE : (t + 1) * WIDE, :], preferred_element_type=jnp.float32)
        out_ref[half] = total


def multiply(own, other, piece, first, acc):
    rows = own.shape[1]
    count = piece.shape[0] // WIDE
    step = min(STEP_TILES, count)
    base = first // (PER_TILE * step)
    a_spec = pl.BlockSpec((step, rows, WIDE), lambda i: (base + i, 0, 0))
    acc_spec = pl.BlockSpec((2, rows, HALF), lambda i: (0, 0, 0))
    extra = [] if acc is None else [acc]
    return pl.pallas_call(
        functools.partial(multiply_kernel, acc is not None),
        grid=(count // step,),
        in_specs=[a_spec, a_spec, pl.BlockSpec((step * WIDE, HALF), lambda i: (i, 0))] + [acc_spec] * len(extra),
        out_specs=acc_spec,
        out_shape=jax.ShapeDtypeStruct((2, rows, HALF), jnp.float32),
        cost_estimate=pl.CostEstimate(
            flops=2 * 2 * rows * HALF * piece.shape[0], bytes_accessed=2 * rows * piece.shape[0] * 2, transcendentals=0
        ),
        compiler_params=pltpu.CompilerParams(vmem_limit_bytes=8 * MIB),
    )(own, other, piece, *extra)


def near_pairs(stage, by):
    ids = np.arange(np.prod(DIMS)).reshape(DIMS)
    pairs = []
    for core in range(NC):
        along_z = core == stage
        grid = ids[..., core].reshape((NZ, NY) + DIMS[4:6])
        moved = np.roll(grid, -by, axis=0 if along_z else 1)
        pairs += list(zip(grid.ravel().tolist(), moved.ravel().tolist()))
    return sorted(pairs)


def near_shift(x, stage, by):
    return lax.ppermute(x, AXES, near_pairs(stage, by))


def gather_near(x, stage):
    h = x.shape[0] // 2
    first, second, x = lax.optimization_barrier((x[:h], x[h:], x))
    minus, plus = near_shift(x, stage, 1), near_shift(x, stage, -1)
    return minus, plus, near_shift(first, stage, 2), near_shift(second, stage, -2)


def place_of(delta, low):
    w = (delta + low) % NEAR - low
    return jnp.where(w == 0, 0, jnp.where(w == -1, 1, jnp.where(w == 1, 2, 3)))


def positions(masked):
    q = masked
    z, y, xh = q // (NY * NXH), (q // NXH) % NY, q % NXH
    low = 2 - xh
    by_z = place_of((z - lax.axis_index(Z)) % NZ, low)
    by_y = place_of((y - lax.axis_index(Y)) % NY, low)
    core = lax.axis_index("c")
    first = jnp.where(core == 0, by_z, by_y)
    second = jnp.where(core == 0, by_y, by_z)
    pos = second * 64 + xh * 32 + first * 8 + (z // NEAR) * NYF + y // NEAR
    return jnp.where(q < CLUSTERS, pos, CLUSTERS).astype(jnp.int32)


def per_device(x_panel, b_panel, a_blocks, a_inner, a_count):
    rows, _, slots, bs, _ = a_blocks.shape
    xh = lax.axis_index("xh")
    live = lax.broadcasted_iota(jnp.int32, a_inner.shape, 2) < a_count[:, :, None]
    masked = jnp.where(live, a_inner, CLUSTERS)

    far = NZF * NYF
    sent = jnp.concatenate(
        [jnp.broadcast_to(b_panel[None, :, h * HALF : (h + 1) * HALF], (far, bs, HALF)) for h in range(NXH)]
    )
    packed = pack(a_blocks, masked)
    sent, packed = lax.optimization_barrier((sent, packed))
    packed_other = lax.ppermute(packed, "xh", [(0, 1), (1, 0)])
    block = lax.all_to_all(sent, ("xh", "zf", "yf"), 0, 0, tiled=False).reshape(-1, HALF)
    own = spread(packed, positions(masked[:, 0, :]))

    block, own = lax.optimization_barrier((block, own))
    h = block.shape[0] // 2
    minus, plus, first, second = gather_near(block, 0)
    plane = jnp.concatenate(
        [block[:h], minus[:h], plus[:h], first, block[h:], minus[h:], plus[h:], second]
    )
    plane, packed_other = lax.optimization_barrier((plane, packed_other))
    pieces = gather_near(plane, 1)

    masked_other = packed_other[:, slots // 2, 0, :slots].astype(jnp.int32)
    other = spread(packed_other, positions(masked_other))
    acc = multiply(own, other, plane, 0, None)
    for piece, at in zip(pieces, (64, 128, 192, 224)):
        acc = multiply(own, other, piece, at, acc)

    ordered = jnp.where(xh == 0, acc, acc[::-1])
    back = lax.all_to_all(ordered.reshape(NXH * rows, bs, HALF), ("xh", "xl", "c"), 0, 0, tiled=False)
    halves = back.reshape(NXH, NXL * NC, bs, HALF).sum(axis=1)
    product = jnp.concatenate([halves[0], halves[1]], axis=-1)
    return (1.5 * x_panel.astype(jnp.float32) - 0.5 * product).astype(jnp.bfloat16)


def solution(mesh):
    fine = Mesh(mesh.devices.reshape(DIMS), AXES)
    grid, layer = Z + Y + ("xh",), ("xl", "c")
    placed = (
        P(grid + layer, None),
        P(grid + layer, None),
        P(grid, layer, None, None, None),
        P(grid, layer, None),
        P(grid, layer),
    )
    return jax.shard_map(
        per_device,
        mesh=fine,
        in_specs=placed,
        out_specs=P(grid + layer, None),
        check_vma=False,
    )
```

time: 373 us -> 135 us (0.36)
  the two profiles are of different devices: /device:TPU:1 before, /device:TPU:16 now
where the time goes in v1:
time: 135 us
  starting transfers between devices  62.9 us (47%)
  waiting for transfers between devices  28.8 us (21%)
  Pallas kernels  20.6 us (15%)
  blocking collectives  11.6 us (9%)
  local copies, waits for them, and re-layouts  7.48 us (6%)
  other arithmetic  2.94 us (2%)
    ppermute x8, starting transfers between devices, near_shift(): return lax.ppermute(x, AXES, near_pairs(stage, by))  32.8 us
    all_to_all x1, starting transfers between devices, per_device(): lax.all_to_all(sent, ('xh', 'zf', 'yf'), 0, 0, tiled=False)  24.8 us
    pallas_call x2, Pallas kernels, spread(): pl.pallas_call(spread_kernel, grid_spec=pltpu.PrefetchScalarGridSpec(num_...  13.9 us
    all_to_all x1, blocking collectives, per_device(): lax.all_to_all(ordered.reshape(NXH * rows, bs, HALF), ('xh', 'xl', 'c'),...  11.6 us
    ppermute x8, waiting for transfers between devices, near_shift(): return lax.ppermute(x, AXES, near_pairs(stage, by))  10.5 us
    all_to_all x1, waiting for transfers between devices, per_device(): lax.all_to_all(sent, ('xh', 'zf', 'yf'), 0, 0, tiled=False)  9.33 us
    ppermute x1, waiting for transfers between devices, per_device(): packed_other = lax.ppermute(packed, 'xh', [(0, 1), (1, 0)])  8.92 us
    pallas_call x5, Pallas kernels, multiply(): pl.pallas_call(functools.partial(multiply_kernel, acc is not None), grid=...  5.85 us
  transfers between devices with their start and end apart: 10, of which 5 were waited for; matrix products, arithmetic and copies ran while one was open for 1% of the time, Pallas kernels for 14%

profile of v1, /device:TPU:16, one launch (start us, length us, event | category | flops | bytes accessed | tf_op | source)
XLA Modules:
  0.0 134.6 jit_solution(3809959748736008166)
XLA Ops:
  0.0 0.7 fusion.43
  0.7 0.8 fusion.16
  1.5 2.2 %copy-done.2 = bf16[4,1,64,64,64]{4,3,2,1,0:T(8,128)(2,1)S(1)} copy-done((bf16[4,1,64,64,64]{4,3,2,1,0:T(8,128)(2,1)S(1)}, bf16[4,1,64,64,64]{4,3,2,1,0:T(8,128)(2,1)}, u32[]{:S(2)}) %copy-start.2) | copy-done | bytes 2097176
  3.7 0.8 shard_map.58.packed_ref
  4.6 0.7 pad_maximum_fusion
  5.4 24.8 %all-to-all-start = ((bf16[16,64,128]{2,1,0:T(8,128)(2,1)}), bf16[16,64,128]{2,1,0:T(8,128)(2,1)S(1)}, u32[]{:S(2)}, u32[]{:S(2)}) async-start(bf16[16,64,128]{2,1,0:T(8,128)(2,1)} %pad_maximum_fusion), calls=%async_computation | async-start | bytes 524288 | tf_op jit(solution)/shard_map/all_to_all | solution.py:179
  30.1 5.3 %collective-permute-start.4 = (bf16[4,33,64,128]{3,2,1,0:T(8,128)(2,1)S(1)}, bf16[4,33,64,128]{3,2,1,0:T(8,128)(2,1)}, u32[]{:S(2)}, u32[]{:S(2)}) collective-permute-start(bf16[4,33,64,128]{3,2,1,0:T(8,128)(2,1)S(1)} %shard_map.58.packed_ref), channel_id=1, source_target_pairs={{0,4},{4,0},{1,5},{5,1},{2,6},{6,2},{3,7},{7,3},{8,12},{12,8},{9,1... | collective-permute-start | bytes 6488072 | tf_op jit(solution)/shard_map/ppermute | solution.py:178
  35.5 6.3 %shard_map.59.own_ref = bf16[65,256,256]{2,1,0:T(8,128)(2,1)S(1)} custom-call(s32[4,64]{1,0:T(4,128)S(1)} %get-tuple-element.29.pos_ref, bf16[4,33,64,128]{3,2,1,0:T(8,128)(2,1)S(1)} %shard_map.58.packed_ref), custom_call_target="tpu_custom_call" | custom-call | bytes 20971520 | tf_op jit(solution)/shard_map/pallas_call | solution.py:76
  41.8 3.3 %copy-done = bf16[65,256,256]{2,1,0:T(8,128)(2,1)} copy-done((bf16[65,256,256]{2,1,0:T(8,128)(2,1)}, bf16[65,256,256]{2,1,0:T(8,128)(2,1)S(1)}, u32[]{:S(2)}) %copy-start) | copy-done | bytes 8519704
  45.1 9.3 %all-to-all-done = bf16[16,64,128]{2,1,0:T(8,128)(2,1)S(1)} async-done(((bf16[16,64,128]{2,1,0:T(8,128)(2,1)}), bf16[16,64,128]{2,1,0:T(8,128)(2,1)S(1)}, u32[]{:S(2)}, u32[]{:S(2)}) %all-to-all-start) | async-done | bytes 262176 | tf_op jit(solution)/shard_map/all_to_all | solution.py:179
  54.5 7.1 %collective-permute-start = (bf16[1024,128]{1,0:T(8,128)(2,1)S(1)}, bf16[1024,128]{1,0:T(8,128)(2,1)S(1)}, u32[]{:S(2)}, u32[]{:S(2)}) collective-permute-start(bf16[1024,128]{1,0:T(8,128)(2,1)S(1)} %bitcast.39), channel_id=1, source_target_pairs={{0,64},{1,9},{2,66},{3,11},{4,68},{5,13},{6,70},{7,15},{8,72},{9,1... | collective-permute-start | bytes 786440 | tf_op jit(solution)/shard_map/ppermute | solution.py:138
  61.6 1.9 %collective-permute-start.1 = (bf16[1024,128]{1,0:T(8,128)(2,1)S(1)}, bf16[1024,128]{1,0:T(8,128)(2,1)S(1)}, u32[]{:S(2)}, u32[]{:S(2)}) collective-permute-start(bf16[1024,128]{1,0:T(8,128)(2,1)S(1)} %bitcast.40), channel_id=1, source_target_pairs={{0,960},{1,57},{2,962},{3,59},{4,964},{5,61},{6,966},{7,63},{8,968... | collective-permute-start | bytes 786440 | tf_op jit(solution)/shard_map/ppermute | solution.py:138
  63.5 3.5 %collective-permute-start.2 = (bf16[512,128]{1,0:T(8,128)(2,1)S(1)}, bf16[512,128]{1,0:T(8,128)(2,1)S(1)}, u32[]{:S(2)}, u32[]{:S(2)}) collective-permute-start(bf16[512,128]{1,0:T(8,128)(2,1)S(1)} %get-tuple-element.22), channel_id=1, source_target_pairs={{0,128},{1,17},{2,130},{3,19},{4,132},{5,21},{6,134},{7,23},{8,136... | collective-permute-start | bytes 393224 | tf_op jit(solution)/shard_map/ppermute | solution.py:138
  67.0 4.4 %collective-permute-start.3 = (bf16[512,128]{1,0:T(8,128)(2,1)S(1)}, bf16[512,128]{1,0:T(8,128)(2,1)S(1)}, u32[]{:S(2)}, u32[]{:S(2)}) collective-permute-start(bf16[512,128]{1,0:T(8,128)(2,1)S(1)} %get-tuple-element.23), channel_id=1, source_target_pairs={{0,896},{1,49},{2,898},{3,51},{4,900},{5,53},{6,902},{7,55},{8,904... | collective-permute-start | bytes 393224 | tf_op jit(solution)/shard_map/ppermute | solution.py:138
  71.6 1.9 %collective-permute-done.2 = bf16[512,128]{1,0:T(8,128)(2,1)S(1)} collective-permute-done((bf16[512,128]{1,0:T(8,128)(2,1)S(1)}, bf16[512,128]{1,0:T(8,128)(2,1)S(1)}, u32[]{:S(2)}, u32[]{:S(2)}) %collective-permute-start.2) | collective-permute-done | bytes 131104 | tf_op jit(solution)/shard_map/ppermute | solution.py:138
  73.5 2.1 %collective-permute-done.3 = bf16[512,128]{1,0:T(8,128)(2,1)S(1)} collective-permute-done((bf16[512,128]{1,0:T(8,128)(2,1)S(1)}, bf16[512,128]{1,0:T(8,128)(2,1)S(1)}, u32[]{:S(2)}, u32[]{:S(2)}) %collective-permute-start.3) | collective-permute-done | bytes 131104 | tf_op jit(solution)/shard_map/ppermute | solution.py:138
  75.7 8.9 %collective-permute-done.4.packed_ref = bf16[4,33,64,128]{3,2,1,0:T(8,128)(2,1)} collective-permute-done((bf16[4,33,64,128]{3,2,1,0:T(8,128)(2,1)S(1)}, bf16[4,33,64,128]{3,2,1,0:T(8,128)(2,1)}, u32[]{:S(2)}, u32[]{:S(2)}) %collective-permute-start.4) | collective-permute-done | bytes 2162720 | tf_op jit(solution)/shard_map/ppermute | solution.py:178
  84.6 1.0 fusion.41
  85.6 2.6 %collective-permute-start.8 = (bf16[4096,128]{1,0:T(8,128)(2,1)S(1)}, bf16[4096,128]{1,0:T(8,128)(2,1)S(1)}, u32[]{:S(2)}, u32[]{:S(2)}) collective-permute-start(bf16[4096,128]{1,0:T(8,128)(2,1)S(1)} %constant_dynamic-update-slice_fusion.b_ref), channel_id=1, source_target_pairs={{0,8},{1,65},{2,10},{3,67},{4,12},{5,69},{6,14},{7,71},{8,16},{9,7... | collective-permute-start | bytes 3145736 | tf_op jit(solution)/shard_map/ppermute | solution.py:138
  88.2 3.3 %collective-permute-start.7 = (bf16[4096,128]{1,0:T(8,128)(2,1)S(1)}, bf16[4096,128]{1,0:T(8,128)(2,1)S(1)}, u32[]{:S(2)}, u32[]{:S(2)}) collective-permute-start(bf16[4096,128]{1,0:T(8,128)(2,1)S(1)} %constant_dynamic-update-slice_fusion.b_ref), channel_id=1, source_target_pairs={{0,56},{1,961},{2,58},{3,963},{4,60},{5,965},{6,62},{7,967},{8,0},... | collective-permute-start | bytes 3145736 | tf_op jit(solution)/shard_map/ppermute | solution.py:138
  91.5 8.1 %collective-permute-start.6 = (bf16[2048,128]{1,0:T(8,128)(2,1)}, bf16[2048,128]{1,0:T(8,128)(2,1)S(1)}, u32[]{:S(2)}, u32[]{:S(2)}) collective-permute-start(bf16[2048,128]{1,0:T(8,128)(2,1)} %get-tuple-element.27), channel_id=1, source_target_pairs={{0,16},{1,129},{2,18},{3,131},{4,20},{5,133},{6,22},{7,135},{8,24}... | collective-permute-start | bytes 1572872 | tf_op jit(solution)/shard_map/ppermute | solution.py:138
  99.6 1.9 %collective-permute-start.5 = (bf16[2048,128]{1,0:T(8,128)(2,1)}, bf16[2048,128]{1,0:T(8,128)(2,1)S(1)}, u32[]{:S(2)}, u32[]{:S(2)}) collective-permute-start(bf16[2048,128]{1,0:T(8,128)(2,1)} %get-tuple-element.26), channel_id=1, source_target_pairs={{0,48},{1,897},{2,50},{3,899},{4,52},{5,901},{6,54},{7,903},{8,56}... | collective-permute-start | bytes 1572872 | tf_op jit(solution)/shard_map/ppermute | solution.py:138
  101.5 0.7 slice_convert_fusion
  102.2 7.6 %shard_map.60.other_ref = bf16[65,256,256]{2,1,0:T(8,128)(2,1)S(1)} custom-call(s32[4,64]{1,0:T(4,128)S(1)} %fusion.32.pos_ref, bf16[4,33,64,128]{3,2,1,0:T(8,128)(2,1)} %collective-permute-done.4.packed_ref), custom_call_target="tpu_custom_call" | custom-call | bytes 20971520 | tf_op jit(solution)/shard_map/pallas_call | solution.py:76
  109.9 1.5 %shard_map.61.rest_0_ = f32[2,256,128]{2,1,0:T(8,128)S(1)} custom-call(bf16[65,256,256]{2,1,0:T(8,128)(2,1)S(1)} %copy-done.1, bf16[65,256,256]{2,1,0:T(8,128)(2,1)S(1)} %shard_map.60.other_ref, bf16[4096,128]{1,0:T(8,128)(2,1)S(1)} %constant_dynamic-update-slice_fusion.b_ref), custom_call_target="tpu_custom_call" | custom-call | flops 536870912 | bytes 4194304 | tf_op jit(solution)/shard_map/pallas_call | solution.py:113
  111.4 1.5 %shard_map.62.rest_0_ = f32[2,256,128]{2,1,0:T(8,128)S(1)} custom-call(bf16[65,256,256]{2,1,0:T(8,128)(2,1)S(1)} %copy-done.1, bf16[65,256,256]{2,1,0:T(8,128)(2,1)S(1)} %shard_map.60.other_ref, bf16[4096,128]{1,0:T(8,128)(2,1)S(1)} %collective-permute-done.8.b_ref, f32[2,256,128]{2,1,0:T(8,128)S(1)} %shard_map.61.rest_0_), custom_call_target="tpu_custom_call" | custom-call | flops 536870912 | bytes 4194304 | tf_op jit(solution)/shard_map/pallas_call | solution.py:113
  112.9 1.5 %shard_map.63.rest_0_ = f32[2,256,128]{2,1,0:T(8,128)S(1)} custom-call(bf16[65,256,256]{2,1,0:T(8,128)(2,1)S(1)} %copy-done.1, bf16[65,256,256]{2,1,0:T(8,128)(2,1)S(1)} %shard_map.60.other_ref, bf16[4096,128]{1,0:T(8,128)(2,1)S(1)} %collective-permute-done.7.b_ref, f32[2,256,128]{2,1,0:T(8,128)S(1)} %shard_map.62.rest_0_), custom_call_target="tpu_custom_call" | custom-call | flops 536870912 | bytes 4194304 | tf_op jit(solution)/shard_map/pallas_call | solution.py:113
  114.4 0.7 shard_map.64.rest_0_
  115.1 6.5 %collective-permute-done.5.b_ref = bf16[2048,128]{1,0:T(8,128)(2,1)S(1)} collective-permute-done((bf16[2048,128]{1,0:T(8,128)(2,1)}, bf16[2048,128]{1,0:T(8,128)(2,1)S(1)}, u32[]{:S(2)}, u32[]{:S(2)}) %collective-permute-start.5) | collective-permute-done | bytes 524320 | tf_op jit(solution)/shard_map/ppermute | solution.py:138
  121.6 0.7 shard_map.65
  122.3 11.6 %all_to_all.10 = f32[8,64,128]{2,1,0:T(8,128)S(1)} all-to-all(f32[8,64,128]{2,1,0:T(8,128)S(1)} %bitcast.42), channel_id=1, replica_groups=mesh['zf'=4,'zn'=4,'yf'=2,'yn'=4,'xh'=2,'xl'=2,'c'=2] {'xh','xl','c'}, dimensions={0} | all-to-all | bytes 524288 | tf_op jit(solution)/shard_map/all_to_all | solution.py:198
  134.0 0.6 fusion.1
  (25 shorter events, 0.3 us)
Async XLA Ops:
  1.5 2.2 %copy-start.2 = (bf16[4,1,64,64,64]{4,3,2,1,0:T(8,128)(2,1)S(1)}, bf16[4,1,64,64,64]{4,3,2,1,0:T(8,128)(2,1)}, u32[]{:S(2)}) copy-start(bf16[4,1,64,64,64]{4,3,2,1,0:T(8,128)(2,1)} %a_ref.1) | copy-start | bytes 6291460
  5.4 49.1 %all-to-all-start = ((bf16[16,64,128]{2,1,0:T(8,128)(2,1)}), bf16[16,64,128]{2,1,0:T(8,128)(2,1)S(1)}, u32[]{:S(2)}, u32[]{:S(2)}) async-start(bf16[16,64,128]{2,1,0:T(8,128)(2,1)} %pad_maximum_fusion), calls=%async_computation | async-start | bytes 524288 | tf_op jit(solution)/shard_map/all_to_all | solution.py:179
  30.1 54.5 %collective-permute-start.4 = (bf16[4,33,64,128]{3,2,1,0:T(8,128)(2,1)S(1)}, bf16[4,33,64,128]{3,2,1,0:T(8,128)(2,1)}, u32[]{:S(2)}, u32[]{:S(2)}) collective-permute-start(bf16[4,33,64,128]{3,2,1,0:T(8,128)(2,1)S(1)} %shard_map.58.packed_ref), channel_id=1, source_target_pairs={{0,4},{4,0},{1,5},{5,1},{2,6},{6,2},{3,7},{7,3},{8,12},{12,8},{9,1... | collective-permute-start | bytes 6488072 | tf_op jit(solution)/shard_map/ppermute | solution.py:178
  41.8 3.3 %copy-start = (bf16[65,256,256]{2,1,0:T(8,128)(2,1)}, bf16[65,256,256]{2,1,0:T(8,128)(2,1)S(1)}, u32[]{:S(2)}) copy-start(bf16[65,256,256]{2,1,0:T(8,128)(2,1)S(1)} %shard_map.59.own_ref) | copy-start | bytes 25559044
  54.5 17.0 %collective-permute-start = (bf16[1024,128]{1,0:T(8,128)(2,1)S(1)}, bf16[1024,128]{1,0:T(8,128)(2,1)S(1)}, u32[]{:S(2)}, u32[]{:S(2)}) collective-permute-start(bf16[1024,128]{1,0:T(8,128)(2,1)S(1)} %bitcast.39), channel_id=1, source_target_pairs={{0,64},{1,9},{2,66},{3,11},{4,68},{5,13},{6,70},{7,15},{8,72},{9,1... | collective-permute-start | bytes 786440 | tf_op jit(solution)/shard_map/ppermute | solution.py:138
  61.6 9.9 %collective-permute-start.1 = (bf16[1024,128]{1,0:T(8,128)(2,1)S(1)}, bf16[1024,128]{1,0:T(8,128)(2,1)S(1)}, u32[]{:S(2)}, u32[]{:S(2)}) collective-permute-start(bf16[1024,128]{1,0:T(8,128)(2,1)S(1)} %bitcast.40), channel_id=1, source_target_pairs={{0,960},{1,57},{2,962},{3,59},{4,964},{5,61},{6,966},{7,63},{8,968... | collective-permute-start | bytes 786440 | tf_op jit(solution)/shard_map/ppermute | solution.py:138
  63.5 9.9 %collective-permute-start.2 = (bf16[512,128]{1,0:T(8,128)(2,1)S(1)}, bf16[512,128]{1,0:T(8,128)(2,1)S(1)}, u32[]{:S(2)}, u32[]{:S(2)}) collective-permute-start(bf16[512,128]{1,0:T(8,128)(2,1)S(1)} %get-tuple-element.22), channel_id=1, source_target_pairs={{0,128},{1,17},{2,130},{3,19},{4,132},{5,21},{6,134},{7,23},{8,136... | collective-permute-start | bytes 393224 | tf_op jit(solution)/shard_map/ppermute | solution.py:138
  67.0 8.6 %collective-permute-start.3 = (bf16[512,128]{1,0:T(8,128)(2,1)S(1)}, bf16[512,128]{1,0:T(8,128)(2,1)S(1)}, u32[]{:S(2)}, u32[]{:S(2)}) collective-permute-start(bf16[512,128]{1,0:T(8,128)(2,1)S(1)} %get-tuple-element.23), channel_id=1, source_target_pairs={{0,896},{1,49},{2,898},{3,51},{4,900},{5,53},{6,902},{7,55},{8,904... | collective-permute-start | bytes 393224 | tf_op jit(solution)/shard_map/ppermute | solution.py:138
  85.6 25.8 %collective-permute-start.8 = (bf16[4096,128]{1,0:T(8,128)(2,1)S(1)}, bf16[4096,128]{1,0:T(8,128)(2,1)S(1)}, u32[]{:S(2)}, u32[]{:S(2)}) collective-permute-start(bf16[4096,128]{1,0:T(8,128)(2,1)S(1)} %constant_dynamic-update-slice_fusion.b_ref), channel_id=1, source_target_pairs={{0,8},{1,65},{2,10},{3,67},{4,12},{5,69},{6,14},{7,71},{8,16},{9,7... | collective-permute-start | bytes 3145736 | tf_op jit(solution)/shard_map/ppermute | solution.py:138
  88.2 24.7 %collective-permute-start.7 = (bf16[4096,128]{1,0:T(8,128)(2,1)S(1)}, bf16[4096,128]{1,0:T(8,128)(2,1)S(1)}, u32[]{:S(2)}, u32[]{:S(2)}) collective-permute-start(bf16[4096,128]{1,0:T(8,128)(2,1)S(1)} %constant_dynamic-update-slice_fusion.b_ref), channel_id=1, source_target_pairs={{0,56},{1,961},{2,58},{3,963},{4,60},{5,965},{6,62},{7,967},{8,0},... | collective-permute-start | bytes 3145736 | tf_op jit(solution)/shard_map/ppermute | solution.py:138
  91.5 22.9 %collective-permute-start.6 = (bf16[2048,128]{1,0:T(8,128)(2,1)}, bf16[2048,128]{1,0:T(8,128)(2,1)S(1)}, u32[]{:S(2)}, u32[]{:S(2)}) collective-permute-start(bf16[2048,128]{1,0:T(8,128)(2,1)} %get-tuple-element.27), channel_id=1, source_target_pairs={{0,16},{1,129},{2,18},{3,131},{4,20},{5,133},{6,22},{7,135},{8,24}... | collective-permute-start | bytes 1572872 | tf_op jit(solution)/shard_map/ppermute | solution.py:138
  99.6 22.1 %collective-permute-start.5 = (bf16[2048,128]{1,0:T(8,128)(2,1)}, bf16[2048,128]{1,0:T(8,128)(2,1)S(1)}, u32[]{:S(2)}, u32[]{:S(2)}) collective-permute-start(bf16[2048,128]{1,0:T(8,128)(2,1)} %get-tuple-element.26), channel_id=1, source_target_pairs={{0,48},{1,897},{2,50},{3,899},{4,52},{5,901},{6,54},{7,903},{8,56}... | collective-permute-start | bytes 1572872 | tf_op jit(solution)/shard_map/ppermute | solution.py:138
  102.2 7.6 %copy-start.1 = (bf16[65,256,256]{2,1,0:T(8,128)(2,1)S(1)}, bf16[65,256,256]{2,1,0:T(8,128)(2,1)}, u32[]{:S(2)}) copy-start(bf16[65,256,256]{2,1,0:T(8,128)(2,1)} %copy-done) | copy-start | bytes 25559044
  115.1 18.9 %copy-start.3 = (bf16[64,256]{1,0:T(8,128)(2,1)S(1)}, bf16[64,256]{1,0:T(8,128)(2,1)}, u32[]{:S(2)}) copy-start(bf16[64,256]{1,0:T(8,128)(2,1)} %param.5) | copy-start | bytes 98308

commit v2 on v1

--- a/solution.py
+++ b/solution.py
@@ -33,14 +33,14 @@
     out_ref[0, pairs] = jnp.broadcast_to(jnp.concatenate([index, index], axis=-1), (BS, 2 * BS)).astype(out_ref.dtype)
 
 
-def pack(a_blocks, masked):
-    rows, _, slots, bs, _ = a_blocks.shape
+def pack(a_blocks, masked, first, rows):
+    _, _, slots, bs, _ = a_blocks.shape
     return pl.pallas_call(
         pack_kernel,
         grid=(rows,),
         in_specs=[
-            pl.BlockSpec((1, 1, slots), lambda r: (r, 0, 0)),
-            pl.BlockSpec((1, 1, slots, bs, bs), lambda r: (r, 0, 0, 0, 0)),
+            pl.BlockSpec((1, 1, slots), lambda r: (first + r, 0, 0)),
+            pl.BlockSpec((1, 1, slots, bs, bs), lambda r: (first + r, 0, 0, 0, 0)),
         ],
         out_specs=pl.BlockSpec((1, slots // 2 + 1, bs, 2 * bs), lambda r: (r, 0, 0, 0)),
         out_shape=jax.ShapeDtypeStruct((rows, slots // 2 + 1, bs, 2 * bs), a_blocks.dtype),
@@ -49,42 +49,50 @@
     )(masked, a_blocks)
 
 
-def spread_kernel(pos_ref, packed_ref, out_ref):
+def spread_kernel(split, pos_ref, low_ref, high_ref, out_ref):
     row = pl.program_id(0)
     lane = lax.broadcasted_iota(jnp.int32, (BS, 2 * BS), 1)
     out_ref[...] = jnp.zeros_like(out_ref)
 
-    def one_pair(pair, carry):
-        straight = packed_ref[0, pair]
-        swapped = jnp.concatenate([straight[:, BS:], straight[:, :BS]], axis=-1)
-        for side in range(2):
-            pos = pos_ref[row, 2 * pair + side]
-            tile = pos // PER_TILE
-            within = pos % PER_TILE
-            at = pl.ds(pl.multiple_of((within // 2) * (2 * BS), 2 * BS), 2 * BS)
-            to_side = within % 2
-            value = jnp.where(to_side == side, straight, swapped)
-            mine = (lane >= BS) == (to_side == 1)
-            out_ref[tile, :, at] = jnp.where(mine, value, out_ref[tile, :, at])
-        return carry
-
-    lax.fori_loop(0, packed_ref.shape[1], one_pair, 0, unroll=4)
-
-
-def spread(packed, pos):
-    rows, more, bs, wide = packed.shape
+    def place(packed_ref):
+        def one_pair(pair, carry):
+            straight = packed_ref[0, pair]
+            swapped = jnp.concatenate([straight[:, BS:], straight[:, :BS]], axis=-1)
+            for side in range(2):
+                pos = pos_ref[row, 2 * pair + side]
+                tile = pos // PER_TILE
+                within = pos % PER_TILE
+                at = pl.ds(pl.multiple_of((within // 2) * (2 * BS), 2 * BS), 2 * BS)
+                to_side = within % 2
+                value = jnp.where(to_side == side, straight, swapped)
+                mine = (lane >= BS) == (to_side == 1)
+                out_ref[tile, :, at] = jnp.where(mine, value, out_ref[tile, :, at])
+            return carry
+
+        lax.fori_loop(0, packed_ref.shape[1], one_pair, 0, unroll=4)
+
+    pl.when(row < split)(lambda: place(low_ref))
+    pl.when(row >= split)(lambda: place(high_ref))
+
+
+def spread(low, high, pos):
+    split, more, bs, wide = low.shape
+    rows = split + high.shape[0]
     return pl.pallas_call(
-        spread_kernel,
+        functools.partial(spread_kernel, split),
         grid_spec=pltpu.PrefetchScalarGridSpec(
             num_scalar_prefetch=1,
             grid=(rows,),
-            in_specs=[pl.BlockSpec((1, more - 1, bs, wide), lambda r, pos: (r, 0, 0, 0))],
+            in_specs=[
+                pl.BlockSpec((1, more - 1, bs, wide), lambda r, pos: (jnp.minimum(r, split - 1), 0, 0, 0)),
+                pl.BlockSpec((1, more - 1, bs, wide), lambda r, pos: (jnp.maximum(r - split, 0), 0, 0, 0)),
+            ],
             out_specs=pl.BlockSpec((TILES + 1, bs, WIDE), lambda r, pos: (0, r, 0)),
         ),
-        out_shape=jax.ShapeDtypeStruct((TILES + 1, rows * bs, WIDE), packed.dtype),
+        out_shape=jax.ShapeDtypeStruct((TILES + 1, rows * bs, WIDE), low.dtype),
         cost_estimate=pl.CostEstimate(flops=0, bytes_accessed=20 * MIB, transcendentals=0),
-        compiler_params=pltpu.CompilerParams(vmem_limit_bytes=8 * MIB),
-    )(pos, packed)
+        compiler_params=pltpu.CompilerParams(vmem_limit_bytes=9 * MIB),
+    )(pos, low, high)
 
 
 def multiply_kernel(has_acc, own_ref, other_ref, b_ref, *rest):
@@ -138,11 +146,12 @@
     return lax.ppermute(x, AXES, near_pairs(stage, by))
 
 
-def gather_near(x, stage):
+def gather_near(x, stage, beside=()):
     h = x.shape[0] // 2
     first, second, x = lax.optimization_barrier((x[:h], x[h:], x))
-    minus, plus = near_shift(x, stage, 1), near_shift(x, stage, -1)
-    return minus, plus, near_shift(first, stage, 2), near_shift(second, stage, -2)
+    minus, plus, first = near_shift(x, stage, 1), near_shift(x, stage, -1), near_shift(first, stage, 2)
+    second, *beside = lax.optimization_barrier((second, *beside))
+    return (minus, plus, first, near_shift(second, stage, -2)), beside
 
 
 def place_of(delta, low):
@@ -153,13 +162,15 @@
 def positions(masked):
     q = masked
     z, y, xh = q // (NY * NXH), (q // NXH) % NY, q % NXH
-    low = 2 - xh
+    zf, yf = z // NEAR, y // NEAR
+    part = zf // 2
+    low = 2 - part
     by_z = place_of((z - lax.axis_index(Z)) % NZ, low)
     by_y = place_of((y - lax.axis_index(Y)) % NY, low)
     core = lax.axis_index("c")
     first = jnp.where(core == 0, by_z, by_y)
     second = jnp.where(core == 0, by_y, by_z)
-    pos = second * 64 + xh * 32 + first * 8 + (z // NEAR) * NYF + y // NEAR
+    pos = second * 64 + part * 32 + first * 8 + (zf % 2) * 4 + yf * NXH + xh
     return jnp.where(q < CLUSTERS, pos, CLUSTERS).astype(jnp.int32)
 
 
@@ -169,27 +180,29 @@
     live = lax.broadcasted_iota(jnp.int32, a_inner.shape, 2) < a_count[:, :, None]
     masked = jnp.where(live, a_inner, CLUSTERS)
 
-    far = NZF * NYF
-    sent = jnp.concatenate(
-        [jnp.broadcast_to(b_panel[None, :, h * HALF : (h + 1) * HALF], (far, bs, HALF)) for h in range(NXH)]
-    )
-    packed = pack(a_blocks, masked)
-    sent, packed = lax.optimization_barrier((sent, packed))
-    packed_other = lax.ppermute(packed, "xh", [(0, 1), (1, 0)])
-    block = lax.all_to_all(sent, ("xh", "zf", "yf"), 0, 0, tiled=False).reshape(-1, HALF)
-    own = spread(packed, positions(masked[:, 0, :]))
+    left, right = b_panel[:, :HALF], b_panel[:, HALF:]
+    got = lax.ppermute(jnp.where(xh == 0, right, left), "xh", [(0, 1), (1, 0)])
+    mine = jnp.where(xh == 0, left, right)
+    pair = jnp.where(xh == 0, jnp.concatenate([mine, got]), jnp.concatenate([got, mine]))
+    split = rows // 2
+    low, high = pack(a_blocks, masked, 0, split), pack(a_blocks, masked, split, rows - split)
+    pair, low, high = lax.optimization_barrier((pair, low, high))
+    low_other = lax.ppermute(low, "xh", [(0, 1), (1, 0)])
+    sent = jnp.broadcast_to(pair[None], (NZF * NYF,) + pair.shape)
+    block = lax.all_to_all(sent, ("zf", "yf"), 0, 0, tiled=False).reshape(-1, HALF)
+    own = spread(low, high, positions(masked[:, 0, :]))
 
     block, own = lax.optimization_barrier((block, own))
     h = block.shape[0] // 2
-    minus, plus, first, second = gather_near(block, 0)
+    (minus, plus, first, second), (low_other, high) = gather_near(block, 0, (low_other, high))
+    high_other = lax.ppermute(high, "xh", [(0, 1), (1, 0)])
     plane = jnp.concatenate(
         [block[:h], minus[:h], plus[:h], first, block[h:], minus[h:], plus[h:], second]
     )
-    plane, packed_other = lax.optimization_barrier((plane, packed_other))
-    pieces = gather_near(plane, 1)
-
-    masked_other = packed_other[:, slots // 2, 0, :slots].astype(jnp.int32)
-    other = spread(packed_other, positions(masked_other))
+    pieces, _ = gather_near(plane, 1)
+
+    masked_other = jnp.concatenate([p[:, slots // 2, 0, :slots] for p in (low_other, high_other)]).astype(jnp.int32)
+    other = spread(low_other, high_other, positions(masked_other))
     acc = multiply(own, other, plane, 0, None)
     for piece, at in zip(pieces, (64, 128, 192, 224)):
         acc = multiply(own, other, piece, at, acc)

time: 135 us -> 121 us (0.90)
  waiting for transfers between devices: 28.8 us -> 15.1 us
  starting transfers between devices: 62.9 us -> 66.8 us
  blocking collectives: 11.6 us -> 10.2 us
    ppermute x1 -> x3, waiting for transfers between devices: 8.92 us -> 3.33 us  [the longest x1 3.33 us: per_device(): high_other = lax.ppermute(high, 'xh', [(0, 1), (1, 0)])]
    ppermute x1 -> x3, starting transfers between devices: 5.33 us -> 10.4 us  [the longest x1 4.92 us: per_device(): got = lax.ppermute(jnp.where(xh == 0, right, left), 'xh', [(0, 1), (1, 0)])]
    ppermute x8, waiting for transfers between devices: 10.5 us -> 5.8 us  [near_shift(): return lax.ppermute(x, AXES, near_pairs(stage, by))]
    all_to_all x1, waiting for transfers between devices: 9.33 us -> 5.92 us  [per_device(): lax.all_to_all(sent, ('zf', 'yf'), 0, 0, tiled=False).reshape(-1, HALF)]
    all_to_all x1, starting transfers between devices: 24.8 us -> 22.2 us  [per_device(): lax.all_to_all(sent, ('zf', 'yf'), 0, 0, tiled=False).reshape(-1, HALF)]
    slice x3 -> x2, local copies, waits for them, and re-layouts: 1.82 us -> 0.01 us  [per_device(): p[:, slots // 2, 0, :slots]]
    all_to_all x1, blocking collectives: 11.6 us -> 10.2 us  [per_device(): lax.all_to_all(ordered.reshape(NXH * rows, bs, HALF), ('xh', 'xl', 'c'),...]
    ppermute x8, starting transfers between devices: 32.8 us -> 34.2 us  [near_shift(): return lax.ppermute(x, AXES, near_pairs(stage, by))]
  transfers between devices with their start and end apart: 10 -> 12, of which waited for: 5 -> 4; matrix products, arithmetic and copies ran while one was open for 1% -> 1% of each run, Pallas kernels for 14% -> 15%
where the time goes in v2:
time: 121 us
  starting transfers between devices  66.8 us (55%)
  Pallas kernels  19.3 us (16%)
  waiting for transfers between devices  15.1 us (12%)
  blocking collectives  10.2 us (8%)
  local copies, waits for them, and re-layouts  6.57 us (5%)
  other arithmetic  2.35 us (2%)
    ppermute x8, starting transfers between devices, near_shift(): return lax.ppermute(x, AXES, near_pairs(stage, by))  34.2 us
    all_to_all x1, starting transfers between devices, per_device(): lax.all_to_all(sent, ('zf', 'yf'), 0, 0, tiled=False).reshape(-1, HALF)  22.2 us
    pallas_call x2, Pallas kernels, spread(): pl.pallas_call(functools.partial(spread_kernel, split), grid_spec=pltpu.P...  12.7 us
    all_to_all x1, blocking collectives, per_device(): lax.all_to_all(ordered.reshape(NXH * rows, bs, HALF), ('xh', 'xl', 'c'),...  10.2 us
    all_to_all x1, waiting for transfers between devices, per_device(): lax.all_to_all(sent, ('zf', 'yf'), 0, 0, tiled=False).reshape(-1, HALF)  5.92 us
    pallas_call x5, Pallas kernels, multiply(): pl.pallas_call(functools.partial(multiply_kernel, acc is not None), grid=...  5.81 us
    ppermute x8, waiting for transfers between devices, near_shift(): return lax.ppermute(x, AXES, near_pairs(stage, by))  5.8 us
    unnamed x17, local copies, waits for them, and re-layouts  5.76 us
  transfers between devices with their start and end apart: 12, of which 4 were waited for; matrix products, arithmetic and copies ran while one was open for 1% of the time, Pallas kernels for 15%

profile of v2, /device:TPU:16, one launch (start us, length us, event | category | flops | bytes accessed | tf_op | source)
XLA Modules:
  0.0 120.6 jit_solution(9852617882200475985)
XLA Ops:
  0.0 0.7 broadcast_select_fusion.1
  0.7 4.9 %collective-permute-start = (bf16[64,128]{1,0:T(8,128)(2,1)S(1)}, bf16[64,128]{1,0:T(8,128)(2,1)S(1)}, u32[]{:S(2)}, u32[]{:S(2)}) collective-permute-start(bf16[64,128]{1,0:T(8,128)(2,1)S(1)} %get-tuple-element.47), channel_id=1, source_target_pairs={{0,4},{4,0},{1,5},{5,1},{2,6},{6,2},{3,7},{7,3},{8,12},{12,8},{9,1... | collective-permute-start | bytes 49160 | tf_op jit(solution)/shard_map/ppermute | solution.py:184
  5.7 0.8 fusion.17
  6.5 2.2 %copy-done.2 = bf16[4,1,64,64,64]{4,3,2,1,0:T(8,128)(2,1)S(1)} copy-done((bf16[4,1,64,64,64]{4,3,2,1,0:T(8,128)(2,1)S(1)}, bf16[4,1,64,64,64]{4,3,2,1,0:T(8,128)(2,1)}, u32[]{:S(2)}) %copy-start.2) | copy-done | bytes 2097176
  8.7 0.4 shard_map.58.low_ref
  9.1 0.4 shard_map.59.high_ref
  9.6 0.8 broadcast_in_dim.34
  10.4 22.2 %all-to-all-start = ((bf16[8,128,128]{2,1,0:T(8,128)(2,1)}), bf16[8,128,128]{2,1,0:T(8,128)(2,1)S(1)}, u32[]{:S(2)}, u32[]{:S(2)}) async-start(bf16[8,128,128]{2,1,0:T(8,128)(2,1)} %broadcast_in_dim.34), calls=%async_computation | async-start | bytes 524288 | tf_op jit(solution)/shard_map/all_to_all | solution.py:192
  32.6 3.2 %collective-permute-start.1 = (bf16[2,33,64,128]{3,2,1,0:T(8,128)(2,1)S(1)}, bf16[2,33,64,128]{3,2,1,0:T(8,128)(2,1)S(1)}, u32[]{:S(2)}, u32[]{:S(2)}) collective-permute-start(bf16[2,33,64,128]{3,2,1,0:T(8,128)(2,1)S(1)} %shard_map.58.low_ref), channel_id=1, source_target_pairs={{0,4},{4,0},{1,5},{5,1},{2,6},{6,2},{3,7},{7,3},{8,12},{12,8},{9,1... | collective-permute-start | bytes 3244040 | tf_op jit(solution)/shard_map/ppermute | solution.py:190
  35.8 6.3 %shard_map.60.own_ref = bf16[65,256,256]{2,1,0:T(8,128)(2,1)S(1)} custom-call(s32[4,64]{1,0:T(4,128)S(1)} %get-tuple-element.33.pos_ref, bf16[2,33,64,128]{3,2,1,0:T(8,128)(2,1)S(1)} %shard_map.58.low_ref, bf16[2,33,64,128]{3,2,1,0:T(8,128)(2,1)S(1)} %shard_map.59.high_ref), custom_call_target="tpu_custom_call" | custom-call | bytes 20971520 | tf_op jit(solution)/shard_map/pallas_call | solution.py:81
  42.1 3.3 %copy-done = bf16[65,256,256]{2,1,0:T(8,128)(2,1)} copy-done((bf16[65,256,256]{2,1,0:T(8,128)(2,1)}, bf16[65,256,256]{2,1,0:T(8,128)(2,1)S(1)}, u32[]{:S(2)}) %copy-start) | copy-done | bytes 8519704
  45.4 5.9 %all-to-all-done = bf16[8,128,128]{2,1,0:T(8,128)(2,1)S(1)} async-done(((bf16[8,128,128]{2,1,0:T(8,128)(2,1)}), bf16[8,128,128]{2,1,0:T(8,128)(2,1)S(1)}, u32[]{:S(2)}, u32[]{:S(2)}) %all-to-all-start) | async-done | bytes 262176 | tf_op jit(solution)/shard_map/all_to_all | solution.py:192
  51.4 5.8 %collective-permute-start.3 = (bf16[1024,128]{1,0:T(8,128)(2,1)S(1)}, bf16[1024,128]{1,0:T(8,128)(2,1)S(1)}, u32[]{:S(2)}, u32[]{:S(2)}) collective-permute-start(bf16[1024,128]{1,0:T(8,128)(2,1)S(1)} %bitcast.45), channel_id=1, source_target_pairs={{0,64},{1,9},{2,66},{3,11},{4,68},{5,13},{6,70},{7,15},{8,72},{9,1... | collective-permute-start | bytes 786440 | tf_op jit(solution)/shard_map/ppermute | solution.py:146
  57.3 5.9 %collective-permute-start.4 = (bf16[1024,128]{1,0:T(8,128)(2,1)S(1)}, bf16[1024,128]{1,0:T(8,128)(2,1)S(1)}, u32[]{:S(2)}, u32[]{:S(2)}) collective-permute-start(bf16[1024,128]{1,0:T(8,128)(2,1)S(1)} %bitcast.46), channel_id=1, source_target_pairs={{0,960},{1,57},{2,962},{3,59},{4,964},{5,61},{6,966},{7,63},{8,968... | collective-permute-start | bytes 786440 | tf_op jit(solution)/shard_map/ppermute | solution.py:146
  63.2 1.9 %collective-permute-start.5 = (bf16[512,128]{1,0:T(8,128)(2,1)S(1)}, bf16[512,128]{1,0:T(8,128)(2,1)S(1)}, u32[]{:S(2)}, u32[]{:S(2)}) collective-permute-start(bf16[512,128]{1,0:T(8,128)(2,1)S(1)} %get-tuple-element.28), channel_id=1, source_target_pairs={{0,128},{1,17},{2,130},{3,19},{4,132},{5,21},{6,134},{7,23},{8,136... | collective-permute-start | bytes 393224 | tf_op jit(solution)/shard_map/ppermute | solution.py:146
  65.2 6.0 %collective-permute-start.6 = (bf16[512,128]{1,0:T(8,128)(2,1)S(1)}, bf16[512,128]{1,0:T(8,128)(2,1)S(1)}, u32[]{:S(2)}, u32[]{:S(2)}) collective-permute-start(bf16[512,128]{1,0:T(8,128)(2,1)S(1)} %get-tuple-element.29), channel_id=1, source_target_pairs={{0,896},{1,49},{2,898},{3,51},{4,900},{5,53},{6,902},{7,55},{8,904... | collective-permute-start | bytes 393224 | tf_op jit(solution)/shard_map/ppermute | solution.py:146
  71.2 2.2 %collective-permute-start.2 = (bf16[2,33,64,128]{3,2,1,0:T(8,128)(2,1)S(1)}, bf16[2,33,64,128]{3,2,1,0:T(8,128)(2,1)S(1)}, u32[]{:S(2)}, u32[]{:S(2)}) collective-permute-start(bf16[2,33,64,128]{3,2,1,0:T(8,128)(2,1)S(1)} %shard_map.59.high_ref), channel_id=1, source_target_pairs={{0,4},{4,0},{1,5},{5,1},{2,6},{6,2},{3,7},{7,3},{8,12},{12,8},{9,1... | collective-permute-start | bytes 3244040 | tf_op jit(solution)/shard_map/ppermute | solution.py:198
  73.7 0.6 collective-permute-done.6
  74.4 3.1 %collective-permute-start.10 = (bf16[4096,128]{1,0:T(8,128)(2,1)S(1)}, bf16[4096,128]{1,0:T(8,128)(2,1)S(1)}, u32[]{:S(2)}, u32[]{:S(2)}) collective-permute-start(bf16[4096,128]{1,0:T(8,128)(2,1)S(1)} %constant_dynamic-update-slice_fusion.b_ref), channel_id=1, source_target_pairs={{0,8},{1,65},{2,10},{3,67},{4,12},{5,69},{6,14},{7,71},{8,16},{9,7... | collective-permute-start | bytes 3145736 | tf_op jit(solution)/shard_map/ppermute | solution.py:146
  77.5 2.7 %collective-permute-start.9 = (bf16[4096,128]{1,0:T(8,128)(2,1)S(1)}, bf16[4096,128]{1,0:T(8,128)(2,1)S(1)}, u32[]{:S(2)}, u32[]{:S(2)}) collective-permute-start(bf16[4096,128]{1,0:T(8,128)(2,1)S(1)} %constant_dynamic-update-slice_fusion.b_ref), channel_id=1, source_target_pairs={{0,56},{1,961},{2,58},{3,963},{4,60},{5,965},{6,62},{7,967},{8,0},... | collective-permute-start | bytes 3145736 | tf_op jit(solution)/shard_map/ppermute | solution.py:146
  80.2 6.7 %collective-permute-start.8 = (bf16[2048,128]{1,0:T(8,128)(2,1)S(1)}, bf16[2048,128]{1,0:T(8,128)(2,1)S(1)}, u32[]{:S(2)}, u32[]{:S(2)}) collective-permute-start(bf16[2048,128]{1,0:T(8,128)(2,1)S(1)} %pad_maximum_fusion), channel_id=1, source_target_pairs={{0,16},{1,129},{2,18},{3,131},{4,20},{5,133},{6,22},{7,135},{8,24}... | collective-permute-start | bytes 1572872 | tf_op jit(solution)/shard_map/ppermute | solution.py:146
  87.0 1.9 %collective-permute-start.7 = (bf16[2048,128]{1,0:T(8,128)(2,1)S(1)}, bf16[2048,128]{1,0:T(8,128)(2,1)S(1)}, u32[]{:S(2)}, u32[]{:S(2)}) collective-permute-start(bf16[2048,128]{1,0:T(8,128)(2,1)S(1)} %pad_maximum_fusion.1), channel_id=1, source_target_pairs={{0,48},{1,897},{2,50},{3,899},{4,52},{5,901},{6,54},{7,903},{8,56}... | collective-permute-start | bytes 1572872 | tf_op jit(solution)/shard_map/ppermute | solution.py:146
  88.9 3.3 %collective-permute-done.2.high_ref = bf16[2,33,64,128]{3,2,1,0:T(8,128)(2,1)S(1)} collective-permute-done((bf16[2,33,64,128]{3,2,1,0:T(8,128)(2,1)S(1)}, bf16[2,33,64,128]{3,2,1,0:T(8,128)(2,1)S(1)}, u32[]{:S(2)}, u32[]{:S(2)}) %collective-permute-start.2) | collective-permute-done | bytes 1081376 | tf_op jit(solution)/shard_map/ppermute | solution.py:198
  92.3 6.3 %shard_map.61.other_ref = bf16[65,256,256]{2,1,0:T(8,128)(2,1)S(1)} custom-call(s32[4,64]{1,0:T(4,128)S(1)} %fusion.35.pos_ref, bf16[2,33,64,128]{3,2,1,0:T(8,128)(2,1)S(1)} %collective-permute-done.1.low_ref, bf16[2,33,64,128]{3,2,1,0:T(8,128)(2,1)S(1)} %collective-permute-done.2.high_ref), custom_call_target="tpu_custom_call" | custom-call | bytes 20971520 | tf_op jit(solution)/shard_map/pallas_call | solution.py:81
  98.7 1.4 %shard_map.62.rest_0_ = f32[2,256,128]{2,1,0:T(8,128)S(1)} custom-call(bf16[65,256,256]{2,1,0:T(8,128)(2,1)S(1)} %copy-done.1, bf16[65,256,256]{2,1,0:T(8,128)(2,1)S(1)} %shard_map.61.other_ref, bf16[4096,128]{1,0:T(8,128)(2,1)S(1)} %constant_dynamic-update-slice_fusion.b_ref), custom_call_target="tpu_custom_call" | custom-call | flops 536870912 | bytes 4194304 | tf_op jit(solution)/shard_map/pallas_call | solution.py:121
  100.2 1.5 %shard_map.63.rest_0_ = f32[2,256,128]{2,1,0:T(8,128)S(1)} custom-call(bf16[65,256,256]{2,1,0:T(8,128)(2,1)S(1)} %copy-done.1, bf16[65,256,256]{2,1,0:T(8,128)(2,1)S(1)} %shard_map.61.other_ref, bf16[4096,128]{1,0:T(8,128)(2,1)S(1)} %collective-permute-done.10.b_ref, f32[2,256,128]{2,1,0:T(8,128)S(1)} %shard_map.62.rest_0_), custom_call_target="tpu_custom_call" | custom-call | flops 536870912 | bytes 4194304 | tf_op jit(solution)/shard_map/pallas_call | solution.py:121
  101.6 1.5 %shard_map.64.rest_0_ = f32[2,256,128]{2,1,0:T(8,128)S(1)} custom-call(bf16[65,256,256]{2,1,0:T(8,128)(2,1)S(1)} %copy-done.1, bf16[65,256,256]{2,1,0:T(8,128)(2,1)S(1)} %shard_map.61.other_ref, bf16[4096,128]{1,0:T(8,128)(2,1)S(1)} %collective-permute-done.9.b_ref, f32[2,256,128]{2,1,0:T(8,128)S(1)} %shard_map.63.rest_0_), custom_call_target="tpu_custom_call" | custom-call | flops 536870912 | bytes 4194304 | tf_op jit(solution)/shard_map/pallas_call | solution.py:121
  103.1 0.7 shard_map.65.rest_0_
  103.8 5.2 %collective-permute-done.7.b_ref = bf16[2048,128]{1,0:T(8,128)(2,1)S(1)} collective-permute-done((bf16[2048,128]{1,0:T(8,128)(2,1)S(1)}, bf16[2048,128]{1,0:T(8,128)(2,1)S(1)}, u32[]{:S(2)}, u32[]{:S(2)}) %collective-permute-start.7) | collective-permute-done | bytes 524320 | tf_op jit(solution)/shard_map/ppermute | solution.py:146
  109.0 0.7 shard_map.66
  109.8 10.2 %all_to_all.10 = f32[8,64,128]{2,1,0:T(8,128)S(1)} all-to-all(f32[8,64,128]{2,1,0:T(8,128)S(1)} %bitcast.48), channel_id=1, replica_groups=mesh['zf'=4,'zn'=4,'yf'=2,'yn'=4,'xh'=2,'xl'=2,'c'=2] {'xh','xl','c'}, dimensions={0} | all-to-all | bytes 524288 | tf_op jit(solution)/shard_map/all_to_all | solution.py:211
  120.0 0.6 fusion.1
  (33 shorter events, 0.5 us)
Async XLA Ops:
  0.7 8.8 %collective-permute-start = (bf16[64,128]{1,0:T(8,128)(2,1)S(1)}, bf16[64,128]{1,0:T(8,128)(2,1)S(1)}, u32[]{:S(2)}, u32[]{:S(2)}) collective-permute-start(bf16[64,128]{1,0:T(8,128)(2,1)S(1)} %get-tuple-element.47), channel_id=1, source_target_pairs={{0,4},{4,0},{1,5},{5,1},{2,6},{6,2},{3,7},{7,3},{8,12},{12,8},{9,1... | collective-permute-start | bytes 49160 | tf_op jit(solution)/shard_map/ppermute | solution.py:184
  6.5 2.2 %copy-start.2 = (bf16[4,1,64,64,64]{4,3,2,1,0:T(8,128)(2,1)S(1)}, bf16[4,1,64,64,64]{4,3,2,1,0:T(8,128)(2,1)}, u32[]{:S(2)}) copy-start(bf16[4,1,64,64,64]{4,3,2,1,0:T(8,128)(2,1)} %a_ref.3) | copy-start | bytes 6291460
  10.4 41.0 %all-to-all-start = ((bf16[8,128,128]{2,1,0:T(8,128)(2,1)}), bf16[8,128,128]{2,1,0:T(8,128)(2,1)S(1)}, u32[]{:S(2)}, u32[]{:S(2)}) async-start(bf16[8,128,128]{2,1,0:T(8,128)(2,1)} %broadcast_in_dim.34), calls=%async_computation | async-start | bytes 524288 | tf_op jit(solution)/shard_map/all_to_all | solution.py:192
  32.6 32.6 %collective-permute-start.1 = (bf16[2,33,64,128]{3,2,1,0:T(8,128)(2,1)S(1)}, bf16[2,33,64,128]{3,2,1,0:T(8,128)(2,1)S(1)}, u32[]{:S(2)}, u32[]{:S(2)}) collective-permute-start(bf16[2,33,64,128]{3,2,1,0:T(8,128)(2,1)S(1)} %shard_map.58.low_ref), channel_id=1, source_target_pairs={{0,4},{4,0},{1,5},{5,1},{2,6},{6,2},{3,7},{7,3},{8,12},{12,8},{9,1... | collective-permute-start | bytes 3244040 | tf_op jit(solution)/shard_map/ppermute | solution.py:190
  42.1 3.3 %copy-start = (bf16[65,256,256]{2,1,0:T(8,128)(2,1)}, bf16[65,256,256]{2,1,0:T(8,128)(2,1)S(1)}, u32[]{:S(2)}) copy-start(bf16[65,256,256]{2,1,0:T(8,128)(2,1)S(1)} %shard_map.60.own_ref) | copy-start | bytes 25559044
  51.4 22.0 %collective-permute-start.3 = (bf16[1024,128]{1,0:T(8,128)(2,1)S(1)}, bf16[1024,128]{1,0:T(8,128)(2,1)S(1)}, u32[]{:S(2)}, u32[]{:S(2)}) collective-permute-start(bf16[1024,128]{1,0:T(8,128)(2,1)S(1)} %bitcast.45), channel_id=1, source_target_pairs={{0,64},{1,9},{2,66},{3,11},{4,68},{5,13},{6,70},{7,15},{8,72},{9,1... | collective-permute-start | bytes 786440 | tf_op jit(solution)/shard_map/ppermute | solution.py:146
  57.3 16.2 %collective-permute-start.4 = (bf16[1024,128]{1,0:T(8,128)(2,1)S(1)}, bf16[1024,128]{1,0:T(8,128)(2,1)S(1)}, u32[]{:S(2)}, u32[]{:S(2)}) collective-permute-start(bf16[1024,128]{1,0:T(8,128)(2,1)S(1)} %bitcast.46), channel_id=1, source_target_pairs={{0,960},{1,57},{2,962},{3,59},{4,964},{5,61},{6,966},{7,63},{8,968... | collective-permute-start | bytes 786440 | tf_op jit(solution)/shard_map/ppermute | solution.py:146
  63.2 10.3 %collective-permute-start.5 = (bf16[512,128]{1,0:T(8,128)(2,1)S(1)}, bf16[512,128]{1,0:T(8,128)(2,1)S(1)}, u32[]{:S(2)}, u32[]{:S(2)}) collective-permute-start(bf16[512,128]{1,0:T(8,128)(2,1)S(1)} %get-tuple-element.28), channel_id=1, source_target_pairs={{0,128},{1,17},{2,130},{3,19},{4,132},{5,21},{6,134},{7,23},{8,136... | collective-permute-start | bytes 393224 | tf_op jit(solution)/shard_map/ppermute | solution.py:146
  65.2 9.2 %collective-permute-start.6 = (bf16[512,128]{1,0:T(8,128)(2,1)S(1)}, bf16[512,128]{1,0:T(8,128)(2,1)S(1)}, u32[]{:S(2)}, u32[]{:S(2)}) collective-permute-start(bf16[512,128]{1,0:T(8,128)(2,1)S(1)} %get-tuple-element.29), channel_id=1, source_target_pairs={{0,896},{1,49},{2,898},{3,51},{4,900},{5,53},{6,902},{7,55},{8,904... | collective-permute-start | bytes 393224 | tf_op jit(solution)/shard_map/ppermute | solution.py:146
  71.2 21.1 %collective-permute-start.2 = (bf16[2,33,64,128]{3,2,1,0:T(8,128)(2,1)S(1)}, bf16[2,33,64,128]{3,2,1,0:T(8,128)(2,1)S(1)}, u32[]{:S(2)}, u32[]{:S(2)}) collective-permute-start(bf16[2,33,64,128]{3,2,1,0:T(8,128)(2,1)S(1)} %shard_map.59.high_ref), channel_id=1, source_target_pairs={{0,4},{4,0},{1,5},{5,1},{2,6},{6,2},{3,7},{7,3},{8,12},{12,8},{9,1... | collective-permute-start | bytes 3244040 | tf_op jit(solution)/shard_map/ppermute | solution.py:198
  74.4 25.8 %collective-permute-start.10 = (bf16[4096,128]{1,0:T(8,128)(2,1)S(1)}, bf16[4096,128]{1,0:T(8,128)(2,1)S(1)}, u32[]{:S(2)}, u32[]{:S(2)}) collective-permute-start(bf16[4096,128]{1,0:T(8,128)(2,1)S(1)} %constant_dynamic-update-slice_fusion.b_ref), channel_id=1, source_target_pairs={{0,8},{1,65},{2,10},{3,67},{4,12},{5,69},{6,14},{7,71},{8,16},{9,7... | collective-permute-start | bytes 3145736 | tf_op jit(solution)/shard_map/ppermute | solution.py:146
  77.5 24.1 %collective-permute-start.9 = (bf16[4096,128]{1,0:T(8,128)(2,1)S(1)}, bf16[4096,128]{1,0:T(8,128)(2,1)S(1)}, u32[]{:S(2)}, u32[]{:S(2)}) collective-permute-start(bf16[4096,128]{1,0:T(8,128)(2,1)S(1)} %constant_dynamic-update-slice_fusion.b_ref), channel_id=1, source_target_pairs={{0,56},{1,961},{2,58},{3,963},{4,60},{5,965},{6,62},{7,967},{8,0},... | collective-permute-start | bytes 3145736 | tf_op jit(solution)/shard_map/ppermute | solution.py:146
  80.2 22.9 %collective-permute-start.8 = (bf16[2048,128]{1,0:T(8,128)(2,1)S(1)}, bf16[2048,128]{1,0:T(8,128)(2,1)S(1)}, u32[]{:S(2)}, u32[]{:S(2)}) collective-permute-start(bf16[2048,128]{1,0:T(8,128)(2,1)S(1)} %pad_maximum_fusion), channel_id=1, source_target_pairs={{0,16},{1,129},{2,18},{3,131},{4,20},{5,133},{6,22},{7,135},{8,24}... | collective-permute-start | bytes 1572872 | tf_op jit(solution)/shard_map/ppermute | solution.py:146
  87.0 22.1 %collective-permute-start.7 = (bf16[2048,128]{1,0:T(8,128)(2,1)S(1)}, bf16[2048,128]{1,0:T(8,128)(2,1)S(1)}, u32[]{:S(2)}, u32[]{:S(2)}) collective-permute-start(bf16[2048,128]{1,0:T(8,128)(2,1)S(1)} %pad_maximum_fusion.1), channel_id=1, source_target_pairs={{0,48},{1,897},{2,50},{3,899},{4,52},{5,901},{6,54},{7,903},{8,56}... | collective-permute-start | bytes 1572872 | tf_op jit(solution)/shard_map/ppermute | solution.py:146
  92.3 6.4 %copy-start.1 = (bf16[65,256,256]{2,1,0:T(8,128)(2,1)S(1)}, bf16[65,256,256]{2,1,0:T(8,128)(2,1)}, u32[]{:S(2)}) copy-start(bf16[65,256,256]{2,1,0:T(8,128)(2,1)} %copy-done) | copy-start | bytes 25559044
  109.8 10.2 %copy-start.3 = (bf16[64,256]{1,0:T(8,128)(2,1)S(1)}, bf16[64,256]{1,0:T(8,128)(2,1)}, u32[]{:S(2)}) copy-start(bf16[64,256]{1,0:T(8,128)(2,1)} %param.5) | copy-start | bytes 98308

commit v3 on v2

--- a/solution.py
+++ b/solution.py
@@ -49,50 +49,46 @@
     )(masked, a_blocks)
 
 
-def spread_kernel(split, pos_ref, low_ref, high_ref, out_ref):
-    row = pl.program_id(0)
+def spread_kernel(first, pos_ref, packed_ref, *rest):
+    out_ref = rest[-1]
+    row = first + pl.program_id(0)
     lane = lax.broadcasted_iota(jnp.int32, (BS, 2 * BS), 1)
     out_ref[...] = jnp.zeros_like(out_ref)
 
-    def place(packed_ref):
-        def one_pair(pair, carry):
-            straight = packed_ref[0, pair]
-            swapped = jnp.concatenate([straight[:, BS:], straight[:, :BS]], axis=-1)
-            for side in range(2):
-                pos = pos_ref[row, 2 * pair + side]
-                tile = pos // PER_TILE
-                within = pos % PER_TILE
-                at = pl.ds(pl.multiple_of((within // 2) * (2 * BS), 2 * BS), 2 * BS)
-                to_side = within % 2
-                value = jnp.where(to_side == side, straight, swapped)
-                mine = (lane >= BS) == (to_side == 1)
-                out_ref[tile, :, at] = jnp.where(mine, value, out_ref[tile, :, at])
-            return carry
-
-        lax.fori_loop(0, packed_ref.shape[1], one_pair, 0, unroll=4)
-
-    pl.when(row < split)(lambda: place(low_ref))
-    pl.when(row >= split)(lambda: place(high_ref))
-
-
-def spread(low, high, pos):
-    split, more, bs, wide = low.shape
-    rows = split + high.shape[0]
+    def one_pair(pair, carry):
+        straight = packed_ref[0, pair]
+        swapped = jnp.concatenate([straight[:, BS:], straight[:, :BS]], axis=-1)
+        for side in range(2):
+            pos = pos_ref[row, 2 * pair + side]
+            tile = pos // PER_TILE
+            within = pos % PER_TILE
+            at = pl.ds(pl.multiple_of((within // 2) * (2 * BS), 2 * BS), 2 * BS)
+            to_side = within % 2
+            value = jnp.where(to_side == side, straight, swapped)
+            mine = (lane >= BS) == (to_side == 1)
+            out_ref[tile, :, at] = jnp.where(mine, value, out_ref[tile, :, at])
+        return carry
+
+    lax.fori_loop(0, packed_ref.shape[1], one_pair, 0, unroll=4)
+
+
+def spread(packed, pos, first, rows, into=None):
+    here, more, bs, wide = packed.shape
+    extra = [] if into is None else [into]
     return pl.pallas_call(
-        functools.partial(spread_kernel, split),
+        functools.partial(spread_kernel, first),
         grid_spec=pltpu.PrefetchScalarGridSpec(
             num_scalar_prefetch=1,
-            grid=(rows,),
-            in_specs=[
-                pl.BlockSpec((1, more - 1, bs, wide), lambda r, pos: (jnp.minimum(r, split - 1), 0, 0, 0)),
-                pl.BlockSpec((1, more - 1, bs, wide), lambda r, pos: (jnp.maximum(r - split, 0), 0, 0, 0)),
-            ],
-            out_specs=pl.BlockSpec((TILES + 1, bs, WIDE), lambda r, pos: (0, r, 0)),
+            grid=(here,),
+            in_specs=[pl.BlockSpec((1, more - 1, bs, wide), lambda r, pos: (r, 0, 0, 0))]
+            + [pl.BlockSpec(memory_space=pl.ANY)] * len(extra),
+            out_specs=pl.BlockSpec((TILES + 1, bs, WIDE), lambda r, pos: (0, first + r, 0)),
         ),
-        out_shape=jax.ShapeDtypeStruct((TILES + 1, rows * bs, WIDE), low.dtype),
-        cost_estimate=pl.CostEstimate(flops=0, bytes_accessed=20 * MIB, transcendentals=0),
-        compiler_params=pltpu.CompilerParams(vmem_limit_bytes=9 * MIB),
-    )(pos, low, high)
+        out_shape=jax.ShapeDtypeStruct((TILES + 1, rows * bs, WIDE), packed.dtype),
+        input_output_aliases={2: 0} if extra else {},
+        cost_estimate=pl.CostEstimate(flops=0, bytes_accessed=10 * MIB, transcendentals=0),
+        compiler_params=pltpu.CompilerParams(vmem_limit_bytes=8 * MIB),
+    )(pos, packed, *extra)
 
 
 def multiply_kernel(has_acc, own_ref, other_ref, b_ref, *rest):
@@ -186,11 +182,11 @@
     pair = jnp.where(xh == 0, jnp.concatenate([mine, got]), jnp.concatenate([got, mine]))
     split = rows // 2
     low, high = pack(a_blocks, masked, 0, split), pack(a_blocks, masked, split, rows - split)
-    pair, low, high = lax.optimization_barrier((pair, low, high))
     low_other = lax.ppermute(low, "xh", [(0, 1), (1, 0)])
     sent = jnp.broadcast_to(pair[None], (NZF * NYF,) + pair.shape)
     block = lax.all_to_all(sent, ("zf", "yf"), 0, 0, tiled=False).reshape(-1, HALF)
-    own = spread(low, high, positions(masked[:, 0, :]))
+    own_pos = positions(masked[:, 0, :])
+    own = spread(high, own_pos, split, rows, spread(low, own_pos, 0, rows))
 
     block, own = lax.optimization_barrier((block, own))
     h = block.shape[0] // 2
@@ -200,9 +196,15 @@
         [block[:h], minus[:h], plus[:h], first, block[h:], minus[h:], plus[h:], second]
     )
     pieces, _ = gather_near(plane, 1)
-
-    masked_other = jnp.concatenate([p[:, slots // 2, 0, :slots] for p in (low_other, high_other)]).astype(jnp.int32)
-    other = spread(low_other, high_other, positions(masked_other))
+    arrived, low_other = lax.optimization_barrier((pieces[0], low_other))
+    pieces = (arrived,) + pieces[1:]
+
+    def positions_in(p):
+        return positions(p[:, slots // 2, 0, :slots].astype(jnp.int32))
+
+    other = spread(low_other, positions_in(low_other), 0, rows)
+    late = jnp.pad(positions_in(high_other), ((split, 0), (0, 0)))
+    other = spread(high_other, late, split, rows, other)
     acc = multiply(own, other, plane, 0, None)
     for piece, at in zip(pieces, (64, 128, 192, 224)):
         acc = multiply(own, other, piece, at, acc)

time: 121 us -> 127 us (1.050)
  starting transfers between devices: 66.8 us -> 72.4 us
  waiting for transfers between devices: 15.1 us -> 13.7 us
    all_to_all x1, waiting for transfers between devices: 5.92 us -> 0.01 us  [per_device(): lax.all_to_all(sent, ('zf', 'yf'), 0, 0, tiled=False).reshape(-1, HALF)]
    ppermute x8, waiting for transfers between devices: 5.8 us -> 11.5 us  [near_shift(): return lax.ppermute(x, AXES, near_pairs(stage, by))]
    ppermute x1, waiting for transfers between devices: 3.33 us -> 0.01 us  [per_device(): high_other = lax.ppermute(high, 'xh', [(0, 1), (1, 0)])]
    ppermute x1, starting transfers between devices: 2.22 us -> 4.93 us  [per_device(): high_other = lax.ppermute(high, 'xh', [(0, 1), (1, 0)])]
    ppermute x1, waiting for transfers between devices: 0.01 us -> 2.2 us  [per_device(): got = lax.ppermute(jnp.where(xh == 0, right, left), 'xh', [(0, 1), (1, 0)])]
    ppermute x1, starting transfers between devices: 3.22 us -> 4.93 us  [per_device(): low_other = lax.ppermute(low, 'xh', [(0, 1), (1, 0)])]
    pallas_call x2 -> x4, Pallas kernels: 12.7 us -> 13.8 us  [spread(): pl.pallas_call(functools.partial(spread_kernel, first), grid_spec=pltpu.P...]
    unnamed x17 -> x19, local copies, waits for them, and re-layouts: 5.76 us -> 5.75 us
  transfers between devices with their start and end apart: 12 -> 12, of which waited for: 4 -> 4; matrix products, arithmetic and copies ran while one was open for 1% -> 1% of each run, Pallas kernels for 15% -> 16%
where the time goes in v3:
time: 127 us; the launch traced here: 126 us
  starting transfers between devices  72.4 us (57%)
  Pallas kernels  20.5 us (16%)
  waiting for transfers between devices  13.7 us (11%)
  blocking collectives  9.95 us (8%)
  local copies, waits for them, and re-layouts  6.54 us (5%)
  other arithmetic  2.4 us (2%)
    ppermute x8, starting transfers between devices, near_shift(): return lax.ppermute(x, AXES, near_pairs(stage, by))  35.4 us
    all_to_all x1, starting transfers between devices, per_device(): lax.all_to_all(sent, ('zf', 'yf'), 0, 0, tiled=False).reshape(-1, HALF)  22.2 us
    pallas_call x4, Pallas kernels, spread(): pl.pallas_call(functools.partial(spread_kernel, first), grid_spec=pltpu.P...  13.8 us
    ppermute x8, waiting for transfers between devices, near_shift(): return lax.ppermute(x, AXES, near_pairs(stage, by))  11.5 us
    all_to_all x1, blocking collectives, per_device(): lax.all_to_all(ordered.reshape(NXH * rows, bs, HALF), ('xh', 'xl', 'c'),...  9.95 us
    pallas_call x5, Pallas kernels, multiply(): pl.pallas_call(functools.partial(multiply_kernel, acc is not None), grid=...  5.77 us
    unnamed x19, local copies, waits for them, and re-layouts  5.75 us
    ppermute x1, starting transfers between devices, per_device(): low_other = lax.ppermute(low, 'xh', [(0, 1), (1, 0)])  4.93 us
  transfers between devices with their start and end apart: 12, of which 4 were waited for; matrix products, arithmetic and copies ran while one was open for 1% of the time, Pallas kernels for 16%

profile of v3, /device:TPU:16, one launch (start us, length us, event | category | flops | bytes accessed | tf_op | source)
XLA Modules:
  0.0 125.9 jit_solution(1723554476878760096)
XLA Ops:
  0.0 0.7 broadcast_select_fusion.1
  0.7 4.9 %collective-permute-start = (bf16[64,128]{1,0:T(8,128)(2,1)S(1)}, bf16[64,128]{1,0:T(8,128)(2,1)S(1)}, u32[]{:S(2)}, u32[]{:S(2)}) collective-permute-start(bf16[64,128]{1,0:T(8,128)(2,1)S(1)} %get-tuple-element.45), channel_id=1, source_target_pairs={{0,4},{4,0},{1,5},{5,1},{2,6},{6,2},{3,7},{7,3},{8,12},{12,8},{9,1... | collective-permute-start | bytes 49160 | tf_op jit(solution)/shard_map/ppermute | solution.py:180
  5.7 2.2 %collective-permute-done = bf16[64,128]{1,0:T(8,128)(2,1)S(1)} collective-permute-done((bf16[64,128]{1,0:T(8,128)(2,1)S(1)}, bf16[64,128]{1,0:T(8,128)(2,1)S(1)}, u32[]{:S(2)}, u32[]{:S(2)}) %collective-permute-start) | collective-permute-done | bytes 16416 | tf_op jit(solution)/shard_map/ppermute | solution.py:180
  7.9 0.8 broadcast_in_dim.46
  8.6 22.2 %all-to-all-start = ((bf16[8,128,128]{2,1,0:T(8,128)(2,1)}), bf16[8,128,128]{2,1,0:T(8,128)(2,1)S(1)}, u32[]{:S(2)}, u32[]{:S(2)}) async-start(bf16[8,128,128]{2,1,0:T(8,128)(2,1)} %broadcast_in_dim.46), calls=%async_computation | async-start | bytes 524288 | tf_op jit(solution)/shard_map/all_to_all | solution.py:187
  30.8 0.8 fusion.17
  31.6 2.2 %copy-done.1 = bf16[4,1,64,64,64]{4,3,2,1,0:T(8,128)(2,1)S(1)} copy-done((bf16[4,1,64,64,64]{4,3,2,1,0:T(8,128)(2,1)S(1)}, bf16[4,1,64,64,64]{4,3,2,1,0:T(8,128)(2,1)}, u32[]{:S(2)}) %copy-start.1) | copy-done | bytes 2097176
  34.2 4.9 %collective-permute-start.1 = (bf16[2,33,64,128]{3,2,1,0:T(8,128)(2,1)S(1)}, bf16[2,33,64,128]{3,2,1,0:T(8,128)(2,1)S(1)}, u32[]{:S(2)}, u32[]{:S(2)}) collective-permute-start(bf16[2,33,64,128]{3,2,1,0:T(8,128)(2,1)S(1)} %shard_map.59.packed_ref), channel_id=1, source_target_pairs={{0,4},{4,0},{1,5},{5,1},{2,6},{6,2},{3,7},{7,3},{8,12},{12,8},{9,1... | collective-permute-start | bytes 3244040 | tf_op jit(solution)/shard_map/ppermute | solution.py:185
  39.6 3.5 %shard_map.60.rest_0_ = bf16[65,256,256]{2,1,0:T(8,128)(2,1)S(1)} custom-call(s32[4,64]{1,0:T(4,128)S(1)} %get-tuple-element.31.pos_ref, bf16[2,33,64,128]{3,2,1,0:T(8,128)(2,1)S(1)} %shard_map.59.packed_ref), custom_call_target="tpu_custom_call" | custom-call | bytes 10485760 | tf_op jit(solution)/shard_map/pallas_call | solution.py:78
  43.1 3.5 %shard_map.61.own_ref = bf16[65,256,256]{2,1,0:T(8,128)(2,1)S(1)} custom-call(s32[4,64]{1,0:T(4,128)S(1)} %get-tuple-element.31.pos_ref, bf16[2,33,64,128]{3,2,1,0:T(8,128)(2,1)S(1)} %shard_map.58.packed_ref, bf16[65,256,256]{2,1,0:T(8,128)(2,1)S(1)} %shard_map.60.rest_0_), custom_call_target="tpu_custom_call", output_to_operand_aliasing={{}: (2, {})} | custom-call | bytes 10485760 | tf_op jit(solution)/shard_map/pallas_call | solution.py:78
  46.6 3.3 %copy-done = bf16[65,256,256]{2,1,0:T(8,128)(2,1)} copy-done((bf16[65,256,256]{2,1,0:T(8,128)(2,1)}, bf16[65,256,256]{2,1,0:T(8,128)(2,1)S(1)}, u32[]{:S(2)}) %copy-start) | copy-done | bytes 8519704
  50.0 4.8 %collective-permute-start.3 = (bf16[1024,128]{1,0:T(8,128)(2,1)S(1)}, bf16[1024,128]{1,0:T(8,128)(2,1)S(1)}, u32[]{:S(2)}, u32[]{:S(2)}) collective-permute-start(bf16[1024,128]{1,0:T(8,128)(2,1)S(1)} %bitcast.43), channel_id=1, source_target_pairs={{0,64},{1,9},{2,66},{3,11},{4,68},{5,13},{6,70},{7,15},{8,72},{9,1... | collective-permute-start | bytes 786440 | tf_op jit(solution)/shard_map/ppermute | solution.py:142
  54.8 5.6 %collective-permute-start.4 = (bf16[1024,128]{1,0:T(8,128)(2,1)S(1)}, bf16[1024,128]{1,0:T(8,128)(2,1)S(1)}, u32[]{:S(2)}, u32[]{:S(2)}) collective-permute-start(bf16[1024,128]{1,0:T(8,128)(2,1)S(1)} %bitcast.44), channel_id=1, source_target_pairs={{0,960},{1,57},{2,962},{3,59},{4,964},{5,61},{6,966},{7,63},{8,968... | collective-permute-start | bytes 786440 | tf_op jit(solution)/shard_map/ppermute | solution.py:142
  60.4 1.9 %collective-permute-start.5 = (bf16[512,128]{1,0:T(8,128)(2,1)S(1)}, bf16[512,128]{1,0:T(8,128)(2,1)S(1)}, u32[]{:S(2)}, u32[]{:S(2)}) collective-permute-start(bf16[512,128]{1,0:T(8,128)(2,1)S(1)} %get-tuple-element.23), channel_id=1, source_target_pairs={{0,128},{1,17},{2,130},{3,19},{4,132},{5,21},{6,134},{7,23},{8,136... | collective-permute-start | bytes 393224 | tf_op jit(solution)/shard_map/ppermute | solution.py:142
  62.4 4.9 %collective-permute-start.2 = (bf16[2,33,64,128]{3,2,1,0:T(8,128)(2,1)S(1)}, bf16[2,33,64,128]{3,2,1,0:T(8,128)(2,1)S(1)}, u32[]{:S(2)}, u32[]{:S(2)}) collective-permute-start(bf16[2,33,64,128]{3,2,1,0:T(8,128)(2,1)S(1)} %shard_map.58.packed_ref), channel_id=1, source_target_pairs={{0,4},{4,0},{1,5},{5,1},{2,6},{6,2},{3,7},{7,3},{8,12},{12,8},{9,1... | collective-permute-start | bytes 3244040 | tf_op jit(solution)/shard_map/ppermute | solution.py:194
  67.3 7.0 %collective-permute-start.6 = (bf16[512,128]{1,0:T(8,128)(2,1)S(1)}, bf16[512,128]{1,0:T(8,128)(2,1)S(1)}, u32[]{:S(2)}, u32[]{:S(2)}) collective-permute-start(bf16[512,128]{1,0:T(8,128)(2,1)S(1)} %get-tuple-element.24), channel_id=1, source_target_pairs={{0,896},{1,49},{2,898},{3,51},{4,900},{5,53},{6,902},{7,55},{8,904... | collective-permute-start | bytes 393224 | tf_op jit(solution)/shard_map/ppermute | solution.py:142
  74.6 3.6 %collective-permute-done.6 = bf16[512,128]{1,0:T(8,128)(2,1)S(1)} collective-permute-done((bf16[512,128]{1,0:T(8,128)(2,1)S(1)}, bf16[512,128]{1,0:T(8,128)(2,1)S(1)}, u32[]{:S(2)}, u32[]{:S(2)}) %collective-permute-start.6) | collective-permute-done | bytes 131104 | tf_op jit(solution)/shard_map/ppermute | solution.py:142
  78.3 2.6 %collective-permute-start.7 = (bf16[4096,128]{1,0:T(8,128)(2,1)S(1)}, bf16[4096,128]{1,0:T(8,128)(2,1)S(1)}, u32[]{:S(2)}, u32[]{:S(2)}) collective-permute-start(bf16[4096,128]{1,0:T(8,128)(2,1)S(1)} %constant_dynamic-update-slice_fusion.b_ref), channel_id=1, source_target_pairs={{0,8},{1,65},{2,10},{3,67},{4,12},{5,69},{6,14},{7,71},{8,16},{9,7... | collective-permute-start | bytes 3145736 | tf_op jit(solution)/shard_map/ppermute | solution.py:142
  80.9 3.3 %collective-permute-start.10 = (bf16[4096,128]{1,0:T(8,128)(2,1)S(1)}, bf16[4096,128]{1,0:T(8,128)(2,1)S(1)}, u32[]{:S(2)}, u32[]{:S(2)}) collective-permute-start(bf16[4096,128]{1,0:T(8,128)(2,1)S(1)} %constant_dynamic-update-slice_fusion.b_ref), channel_id=1, source_target_pairs={{0,56},{1,961},{2,58},{3,963},{4,60},{5,965},{6,62},{7,967},{8,0},... | collective-permute-start | bytes 3145736 | tf_op jit(solution)/shard_map/ppermute | solution.py:142
  84.2 5.3 %collective-permute-start.8 = (bf16[2048,128]{1,0:T(8,128)(2,1)S(1)}, bf16[2048,128]{1,0:T(8,128)(2,1)S(1)}, u32[]{:S(2)}, u32[]{:S(2)}) collective-permute-start(bf16[2048,128]{1,0:T(8,128)(2,1)S(1)} %pad_maximum_fusion.1), channel_id=1, source_target_pairs={{0,48},{1,897},{2,50},{3,899},{4,52},{5,901},{6,54},{7,903},{8,56}... | collective-permute-start | bytes 1572872 | tf_op jit(solution)/shard_map/ppermute | solution.py:142
  89.4 4.9 %collective-permute-start.9 = (bf16[2048,128]{1,0:T(8,128)(2,1)S(1)}, bf16[2048,128]{1,0:T(8,128)(2,1)S(1)}, u32[]{:S(2)}, u32[]{:S(2)}) collective-permute-start(bf16[2048,128]{1,0:T(8,128)(2,1)S(1)} %pad_maximum_fusion), channel_id=1, source_target_pairs={{0,16},{1,129},{2,18},{3,131},{4,20},{5,133},{6,22},{7,135},{8,24}... | collective-permute-start | bytes 1572872 | tf_op jit(solution)/shard_map/ppermute | solution.py:142
  94.4 0.6 collective-permute-done.7.b_ref
  95.1 3.4 %shard_map.62.rest_0_ = bf16[65,256,256]{2,1,0:T(8,128)(2,1)S(1)} custom-call(s32[2,64]{1,0:T(2,128)S(1)} %compare_select_fusion.26.pos_ref, bf16[2,33,64,128]{3,2,1,0:T(8,128)(2,1)S(1)} %collective-permute-done.1.packed_ref), custom_call_target="tpu_custom_call" | custom-call | bytes 10485760 | tf_op jit(solution)/shard_map/pallas_call | solution.py:78
  98.5 3.5 %shard_map.63.other_ref = bf16[65,256,256]{2,1,0:T(8,128)(2,1)S(1)} custom-call(s32[4,64]{1,0:T(4,128)S(1)} %pad.4.pos_ref, bf16[2,33,64,128]{3,2,1,0:T(8,128)(2,1)S(1)} %collective-permute-done.2.packed_ref, bf16[65,256,256]{2,1,0:T(8,128)(2,1)S(1)} %shard_map.62.rest_0_), custom_call_target="tpu_custom_call", output_to_operand_aliasing={{}: (2, {})} | custom-call | bytes 10485760 | tf_op jit(solution)/shard_map/pallas_call | solution.py:78
  102.1 1.5 %shard_map.64.rest_0_ = f32[2,256,128]{2,1,0:T(8,128)S(1)} custom-call(bf16[65,256,256]{2,1,0:T(8,128)(2,1)S(1)} %bitcast.39, bf16[65,256,256]{2,1,0:T(8,128)(2,1)S(1)} %shard_map.63.other_ref, bf16[4096,128]{1,0:T(8,128)(2,1)S(1)} %constant_dynamic-update-slice_fusion.b_ref), custom_call_target="tpu_custom_call" | custom-call | flops 536870912 | bytes 4194304 | tf_op jit(solution)/shard_map/pallas_call | solution.py:117
  103.5 1.5 %shard_map.65.rest_0_ = f32[2,256,128]{2,1,0:T(8,128)S(1)} custom-call(bf16[65,256,256]{2,1,0:T(8,128)(2,1)S(1)} %bitcast.39, bf16[65,256,256]{2,1,0:T(8,128)(2,1)S(1)} %shard_map.63.other_ref, bf16[4096,128]{1,0:T(8,128)(2,1)S(1)} %collective-permute-done.7.b_ref, f32[2,256,128]{2,1,0:T(8,128)S(1)} %shard_map.64.rest_0_), custom_call_target="tpu_custom_call" | custom-call | flops 536870912 | bytes 4194304 | tf_op jit(solution)/shard_map/pallas_call | solution.py:117
  105.0 1.4 %shard_map.66.rest_0_ = f32[2,256,128]{2,1,0:T(8,128)S(1)} custom-call(bf16[65,256,256]{2,1,0:T(8,128)(2,1)S(1)} %bitcast.39, bf16[65,256,256]{2,1,0:T(8,128)(2,1)S(1)} %shard_map.63.other_ref, bf16[4096,128]{1,0:T(8,128)(2,1)S(1)} %collective-permute-done.10.b_ref, f32[2,256,128]{2,1,0:T(8,128)S(1)} %shard_map.65.rest_0_), custom_call_target="tpu_custom_call" | custom-call | flops 536870912 | bytes 4194304 | tf_op jit(solution)/shard_map/pallas_call | solution.py:117
  106.5 0.7 shard_map.67.rest_0_
  107.2 7.3 %collective-permute-done.8.b_ref = bf16[2048,128]{1,0:T(8,128)(2,1)S(1)} collective-permute-done((bf16[2048,128]{1,0:T(8,128)(2,1)S(1)}, bf16[2048,128]{1,0:T(8,128)(2,1)S(1)}, u32[]{:S(2)}, u32[]{:S(2)}) %collective-permute-start.8) | collective-permute-done | bytes 524320 | tf_op jit(solution)/shard_map/ppermute | solution.py:142
  114.5 0.7 shard_map.68
  115.2 9.9 %all_to_all.10 = f32[8,64,128]{2,1,0:T(8,128)S(1)} all-to-all(f32[8,64,128]{2,1,0:T(8,128)S(1)} %bitcast.46), channel_id=1, replica_groups=mesh['zf'=4,'zn'=4,'yf'=2,'yn'=4,'xh'=2,'xl'=2,'c'=2] {'xh','xl','c'}, dimensions={0} | all-to-all | bytes 524288 | tf_op jit(solution)/shard_map/all_to_all | solution.py:213
  125.2 0.6 fusion.1
  (40 shorter events, 1.4 us)
Async XLA Ops:
  0.7 7.1 %collective-permute-start = (bf16[64,128]{1,0:T(8,128)(2,1)S(1)}, bf16[64,128]{1,0:T(8,128)(2,1)S(1)}, u32[]{:S(2)}, u32[]{:S(2)}) collective-permute-start(bf16[64,128]{1,0:T(8,128)(2,1)S(1)} %get-tuple-element.45), channel_id=1, source_target_pairs={{0,4},{4,0},{1,5},{5,1},{2,6},{6,2},{3,7},{7,3},{8,12},{12,8},{9,1... | collective-permute-start | bytes 49160 | tf_op jit(solution)/shard_map/ppermute | solution.py:180
  8.6 41.3 %all-to-all-start = ((bf16[8,128,128]{2,1,0:T(8,128)(2,1)}), bf16[8,128,128]{2,1,0:T(8,128)(2,1)S(1)}, u32[]{:S(2)}, u32[]{:S(2)}) async-start(bf16[8,128,128]{2,1,0:T(8,128)(2,1)} %broadcast_in_dim.46), calls=%async_computation | async-start | bytes 524288 | tf_op jit(solution)/shard_map/all_to_all | solution.py:187
  31.6 2.2 %copy-start.1 = (bf16[4,1,64,64,64]{4,3,2,1,0:T(8,128)(2,1)S(1)}, bf16[4,1,64,64,64]{4,3,2,1,0:T(8,128)(2,1)}, u32[]{:S(2)}) copy-start(bf16[4,1,64,64,64]{4,3,2,1,0:T(8,128)(2,1)} %a_ref.3) | copy-start | bytes 6291460
  34.2 28.1 %collective-permute-start.1 = (bf16[2,33,64,128]{3,2,1,0:T(8,128)(2,1)S(1)}, bf16[2,33,64,128]{3,2,1,0:T(8,128)(2,1)S(1)}, u32[]{:S(2)}, u32[]{:S(2)}) collective-permute-start(bf16[2,33,64,128]{3,2,1,0:T(8,128)(2,1)S(1)} %shard_map.59.packed_ref), channel_id=1, source_target_pairs={{0,4},{4,0},{1,5},{5,1},{2,6},{6,2},{3,7},{7,3},{8,12},{12,8},{9,1... | collective-permute-start | bytes 3244040 | tf_op jit(solution)/shard_map/ppermute | solution.py:185
  46.6 3.3 %copy-start = (bf16[65,256,256]{2,1,0:T(8,128)(2,1)}, bf16[65,256,256]{2,1,0:T(8,128)(2,1)S(1)}, u32[]{:S(2)}) copy-start(bf16[65,256,256]{2,1,0:T(8,128)(2,1)S(1)} %shard_map.61.own_ref) | copy-start | bytes 25559044
  50.0 24.4 %collective-permute-start.3 = (bf16[1024,128]{1,0:T(8,128)(2,1)S(1)}, bf16[1024,128]{1,0:T(8,128)(2,1)S(1)}, u32[]{:S(2)}, u32[]{:S(2)}) collective-permute-start(bf16[1024,128]{1,0:T(8,128)(2,1)S(1)} %bitcast.43), channel_id=1, source_target_pairs={{0,64},{1,9},{2,66},{3,11},{4,68},{5,13},{6,70},{7,15},{8,72},{9,1... | collective-permute-start | bytes 786440 | tf_op jit(solution)/shard_map/ppermute | solution.py:142
  54.8 19.6 %collective-permute-start.4 = (bf16[1024,128]{1,0:T(8,128)(2,1)S(1)}, bf16[1024,128]{1,0:T(8,128)(2,1)S(1)}, u32[]{:S(2)}, u32[]{:S(2)}) collective-permute-start(bf16[1024,128]{1,0:T(8,128)(2,1)S(1)} %bitcast.44), channel_id=1, source_target_pairs={{0,960},{1,57},{2,962},{3,59},{4,964},{5,61},{6,966},{7,63},{8,968... | collective-permute-start | bytes 786440 | tf_op jit(solution)/shard_map/ppermute | solution.py:142
  60.4 14.0 %collective-permute-start.5 = (bf16[512,128]{1,0:T(8,128)(2,1)S(1)}, bf16[512,128]{1,0:T(8,128)(2,1)S(1)}, u32[]{:S(2)}, u32[]{:S(2)}) collective-permute-start(bf16[512,128]{1,0:T(8,128)(2,1)S(1)} %get-tuple-element.23), channel_id=1, source_target_pairs={{0,128},{1,17},{2,130},{3,19},{4,132},{5,21},{6,134},{7,23},{8,136... | collective-permute-start | bytes 393224 | tf_op jit(solution)/shard_map/ppermute | solution.py:142
  62.4 32.0 %collective-permute-start.2 = (bf16[2,33,64,128]{3,2,1,0:T(8,128)(2,1)S(1)}, bf16[2,33,64,128]{3,2,1,0:T(8,128)(2,1)S(1)}, u32[]{:S(2)}, u32[]{:S(2)}) collective-permute-start(bf16[2,33,64,128]{3,2,1,0:T(8,128)(2,1)S(1)} %shard_map.58.packed_ref), channel_id=1, source_target_pairs={{0,4},{4,0},{1,5},{5,1},{2,6},{6,2},{3,7},{7,3},{8,12},{12,8},{9,1... | collective-permute-start | bytes 3244040 | tf_op jit(solution)/shard_map/ppermute | solution.py:194
  67.3 10.9 %collective-permute-start.6 = (bf16[512,128]{1,0:T(8,128)(2,1)S(1)}, bf16[512,128]{1,0:T(8,128)(2,1)S(1)}, u32[]{:S(2)}, u32[]{:S(2)}) collective-permute-start(bf16[512,128]{1,0:T(8,128)(2,1)S(1)} %get-tuple-element.24), channel_id=1, source_target_pairs={{0,896},{1,49},{2,898},{3,51},{4,900},{5,53},{6,902},{7,55},{8,904... | collective-permute-start | bytes 393224 | tf_op jit(solution)/shard_map/ppermute | solution.py:142
  78.3 16.7 %collective-permute-start.7 = (bf16[4096,128]{1,0:T(8,128)(2,1)S(1)}, bf16[4096,128]{1,0:T(8,128)(2,1)S(1)}, u32[]{:S(2)}, u32[]{:S(2)}) collective-permute-start(bf16[4096,128]{1,0:T(8,128)(2,1)S(1)} %constant_dynamic-update-slice_fusion.b_ref), channel_id=1, source_target_pairs={{0,8},{1,65},{2,10},{3,67},{4,12},{5,69},{6,14},{7,71},{8,16},{9,7... | collective-permute-start | bytes 3145736 | tf_op jit(solution)/shard_map/ppermute | solution.py:142
  80.9 24.1 %collective-permute-start.10 = (bf16[4096,128]{1,0:T(8,128)(2,1)S(1)}, bf16[4096,128]{1,0:T(8,128)(2,1)S(1)}, u32[]{:S(2)}, u32[]{:S(2)}) collective-permute-start(bf16[4096,128]{1,0:T(8,128)(2,1)S(1)} %constant_dynamic-update-slice_fusion.b_ref), channel_id=1, source_target_pairs={{0,56},{1,961},{2,58},{3,963},{4,60},{5,965},{6,62},{7,967},{8,0},... | collective-permute-start | bytes 3145736 | tf_op jit(solution)/shard_map/ppermute | solution.py:142
  84.2 30.3 %collective-permute-start.8 = (bf16[2048,128]{1,0:T(8,128)(2,1)S(1)}, bf16[2048,128]{1,0:T(8,128)(2,1)S(1)}, u32[]{:S(2)}, u32[]{:S(2)}) collective-permute-start(bf16[2048,128]{1,0:T(8,128)(2,1)S(1)} %pad_maximum_fusion.1), channel_id=1, source_target_pairs={{0,48},{1,897},{2,50},{3,899},{4,52},{5,901},{6,54},{7,903},{8,56}... | collective-permute-start | bytes 1572872 | tf_op jit(solution)/shard_map/ppermute | solution.py:142
  89.4 17.0 %collective-permute-start.9 = (bf16[2048,128]{1,0:T(8,128)(2,1)S(1)}, bf16[2048,128]{1,0:T(8,128)(2,1)S(1)}, u32[]{:S(2)}, u32[]{:S(2)}) collective-permute-start(bf16[2048,128]{1,0:T(8,128)(2,1)S(1)} %pad_maximum_fusion), channel_id=1, source_target_pairs={{0,16},{1,129},{2,18},{3,131},{4,20},{5,133},{6,22},{7,135},{8,24}... | collective-permute-start | bytes 1572872 | tf_op jit(solution)/shard_map/ppermute | solution.py:142
  95.1 7.0 %slice-start = ((s8[8519680]{0:T(1024)(128)(4,1)}), s8[4194304]{0:T(1024)(128)(4,1)S(1)}, s32[]{:S(2)}) async-start(s8[8519680]{0:T(1024)(128)(4,1)} %bitcast.38), calls=%async_computation.2 | async-start | bytes 8388608
  95.1 7.0 %slice-start.1 = ((s8[8519680]{0:T(1024)(128)(4,1)}), s8[4194304]{0:T(1024)(128)(4,1)S(1)}, s32[]{:S(2)}) async-start(s8[8519680]{0:T(1024)(128)(4,1)} %bitcast.38), calls=%async_computation.3 | async-start | bytes 8388608
  98.5 3.5 %slice-start.2 = ((s8[8519680]{0:T(1024)(128)(4,1)}), s8[131072]{0:T(1024)(128)(4,1)S(1)}, s32[]{:S(2)}) async-start(s8[8519680]{0:T(1024)(128)(4,1)} %bitcast.38), calls=%async_computation.4 | async-start | bytes 262144
  115.2 10.0 %copy-start.2 = (bf16[64,256]{1,0:T(8,128)(2,1)S(1)}, bf16[64,256]{1,0:T(8,128)(2,1)}, u32[]{:S(2)}) copy-start(bf16[64,256]{1,0:T(8,128)(2,1)} %param.5) | copy-start | bytes 98308

commit v4 on v2

--- a/solution.py
+++ b/solution.py
@@ -146,12 +146,11 @@
     return lax.ppermute(x, AXES, near_pairs(stage, by))
 
 
-def gather_near(x, stage, beside=()):
+def gather_near(x, stage):
     h = x.shape[0] // 2
     first, second, x = lax.optimization_barrier((x[:h], x[h:], x))
-    minus, plus, first = near_shift(x, stage, 1), near_shift(x, stage, -1), near_shift(first, stage, 2)
-    second, *beside = lax.optimization_barrier((second, *beside))
-    return (minus, plus, first, near_shift(second, stage, -2)), beside
+    minus, plus = near_shift(x, stage, 1), near_shift(x, stage, -1)
+    return minus, plus, near_shift(first, stage, 2), near_shift(second, stage, -2)
 
 
 def place_of(delta, low):
@@ -165,11 +164,11 @@
     zf, yf = z // NEAR, y // NEAR
     part = zf // 2
     low = 2 - part
-    by_z = place_of((z - lax.axis_index(Z)) % NZ, low)
-    by_y = place_of((y - lax.axis_index(Y)) % NY, low)
+    dz = (z - lax.axis_index(Z)) % NZ
+    dy = (y - lax.axis_index(Y)) % NY
     core = lax.axis_index("c")
-    first = jnp.where(core == 0, by_z, by_y)
-    second = jnp.where(core == 0, by_y, by_z)
+    first = place_of(jnp.where(core == 0, dz, dy), 2)
+    second = place_of(jnp.where(core == 0, dy, dz), low)
     pos = second * 64 + part * 32 + first * 8 + (zf % 2) * 4 + yf * NXH + xh
     return jnp.where(q < CLUSTERS, pos, CLUSTERS).astype(jnp.int32)
 
@@ -194,12 +193,14 @@
 
     block, own = lax.optimization_barrier((block, own))
     h = block.shape[0] // 2
-    (minus, plus, first, second), (low_other, high) = gather_near(block, 0, (low_other, high))
+    twice, minus = near_shift(block, 0, 2), near_shift(block, 0, 1)
+    block, low_other, high = lax.optimization_barrier((block, low_other, high))
+    plus = near_shift(block, 0, -1)
     high_other = lax.ppermute(high, "xh", [(0, 1), (1, 0)])
     plane = jnp.concatenate(
-        [block[:h], minus[:h], plus[:h], first, block[h:], minus[h:], plus[h:], second]
+        [block[:h], minus[:h], plus[:h], twice[:h], block[h:], minus[h:], plus[h:], twice[h:]]
     )
-    pieces, _ = gather_near(plane, 1)
+    pieces = gather_near(plane, 1)
 
     masked_other = jnp.concatenate([p[:, slots // 2, 0, :slots] for p in (low_other, high_other)]).astype(jnp.int32)
     other = spread(low_other, high_other, positions(masked_other))

time: 121 us -> 122 us (level)
  starting transfers between devices: 66.8 us -> 62.8 us
  waiting for transfers between devices: 15.1 us -> 18.9 us
    ppermute x8 -> x7, starting transfers between devices: 34.2 us -> 28.2 us  [near_shift(): return lax.ppermute(x, AXES, near_pairs(stage, by))]
    all_to_all x1, waiting for transfers between devices: 5.92 us -> 8.97 us  [per_device(): lax.all_to_all(sent, ('zf', 'yf'), 0, 0, tiled=False).reshape(-1, HALF)]
    ppermute x8 -> x7, waiting for transfers between devices: 5.8 us -> 8.63 us  [near_shift(): return lax.ppermute(x, AXES, near_pairs(stage, by))]
    ppermute x1, starting transfers between devices: 2.22 us -> 4.3 us  [per_device(): high_other = lax.ppermute(high, 'xh', [(0, 1), (1, 0)])]
    ppermute x1, waiting for transfers between devices: 3.33 us -> 1.34 us  [per_device(): high_other = lax.ppermute(high, 'xh', [(0, 1), (1, 0)])]
  transfers between devices with their start and end apart: 12 -> 11, of which waited for: 4 -> 4; matrix products, arithmetic and copies ran while one was open for 1% -> 2% of each run, Pallas kernels for 15% -> 15%
where the time goes in v4:
time: 122 us; the launch traced here: 121 us
  starting transfers between devices  62.8 us (51%)
  Pallas kernels  19.4 us (16%)
  waiting for transfers between devices  18.9 us (15%)
  blocking collectives  10.7 us (9%)
  local copies, waits for them, and re-layouts  6.59 us (5%)
  other arithmetic  2.34 us (2%)
    ppermute x7, starting transfers between devices, near_shift(): return lax.ppermute(x, AXES, near_pairs(stage, by))  28.2 us
    all_to_all x1, starting transfers between devices, per_device(): lax.all_to_all(sent, ('zf', 'yf'), 0, 0, tiled=False).reshape(-1, HALF)  22.2 us
    pallas_call x2, Pallas kernels, spread(): pl.pallas_call(functools.partial(spread_kernel, split), grid_spec=pltpu.P...  12.7 us
    all_to_all x1, blocking collectives, per_device(): lax.all_to_all(ordered.reshape(NXH * rows, bs, HALF), ('xh', 'xl', 'c'),...  10.7 us
    all_to_all x1, waiting for transfers between devices, per_device(): lax.all_to_all(sent, ('zf', 'yf'), 0, 0, tiled=False).reshape(-1, HALF)  8.97 us
    ppermute x7, waiting for transfers between devices, near_shift(): return lax.ppermute(x, AXES, near_pairs(stage, by))  8.63 us
    pallas_call x5, Pallas kernels, multiply(): pl.pallas_call(functools.partial(multiply_kernel, acc is not None), grid=...  5.88 us
    unnamed x17, local copies, waits for them, and re-layouts  5.75 us
  transfers between devices with their start and end apart: 11, of which 4 were waited for; matrix products, arithmetic and copies ran while one was open for 2% of the time, Pallas kernels for 15%

profile of v4, /device:TPU:16, one launch (start us, length us, event | category | flops | bytes accessed | tf_op | source)
XLA Modules:
  0.0 121.2 jit_solution(3666119470423027354)
XLA Ops:
  0.0 0.7 broadcast_select_fusion.1
  0.7 4.9 %collective-permute-start = (bf16[64,128]{1,0:T(8,128)(2,1)S(1)}, bf16[64,128]{1,0:T(8,128)(2,1)S(1)}, u32[]{:S(2)}, u32[]{:S(2)}) collective-permute-start(bf16[64,128]{1,0:T(8,128)(2,1)S(1)} %get-tuple-element.44), channel_id=1, source_target_pairs={{0,4},{4,0},{1,5},{5,1},{2,6},{6,2},{3,7},{7,3},{8,12},{12,8},{9,1... | collective-permute-start | bytes 49160 | tf_op jit(solution)/shard_map/ppermute | solution.py:183
  5.7 0.8 fusion.15
  6.5 2.2 %copy-done.2 = bf16[4,1,64,64,64]{4,3,2,1,0:T(8,128)(2,1)S(1)} copy-done((bf16[4,1,64,64,64]{4,3,2,1,0:T(8,128)(2,1)S(1)}, bf16[4,1,64,64,64]{4,3,2,1,0:T(8,128)(2,1)}, u32[]{:S(2)}) %copy-start.2) | copy-done | bytes 2097176
  8.7 0.4 shard_map.58.low_ref
  9.1 0.4 shard_map.59.high_ref
  9.6 3.2 %collective-permute-start.1 = (bf16[2,33,64,128]{3,2,1,0:T(8,128)(2,1)S(1)}, bf16[2,33,64,128]{3,2,1,0:T(8,128)(2,1)S(1)}, u32[]{:S(2)}, u32[]{:S(2)}) collective-permute-start(bf16[2,33,64,128]{3,2,1,0:T(8,128)(2,1)S(1)} %shard_map.58.low_ref), channel_id=1, source_target_pairs={{0,4},{4,0},{1,5},{5,1},{2,6},{6,2},{3,7},{7,3},{8,12},{12,8},{9,1... | collective-permute-start | bytes 3244040 | tf_op jit(solution)/shard_map/ppermute | solution.py:189
  12.8 0.8 broadcast_in_dim.34
  13.6 22.2 %all-to-all-start = ((bf16[8,128,128]{2,1,0:T(8,128)(2,1)}), bf16[8,128,128]{2,1,0:T(8,128)(2,1)S(1)}, u32[]{:S(2)}, u32[]{:S(2)}) async-start(bf16[8,128,128]{2,1,0:T(8,128)(2,1)} %broadcast_in_dim.34), calls=%async_computation | async-start | bytes 524288 | tf_op jit(solution)/shard_map/all_to_all | solution.py:191
  35.8 6.3 %shard_map.60.own_ref = bf16[65,256,256]{2,1,0:T(8,128)(2,1)S(1)} custom-call(s32[4,64]{1,0:T(4,128)S(1)} %get-tuple-element.27.pos_ref, bf16[2,33,64,128]{3,2,1,0:T(8,128)(2,1)S(1)} %shard_map.58.low_ref, bf16[2,33,64,128]{3,2,1,0:T(8,128)(2,1)S(1)} %shard_map.59.high_ref), custom_call_target="tpu_custom_call" | custom-call | bytes 20971520 | tf_op jit(solution)/shard_map/pallas_call | solution.py:81
  42.1 3.3 %copy-done = bf16[65,256,256]{2,1,0:T(8,128)(2,1)} copy-done((bf16[65,256,256]{2,1,0:T(8,128)(2,1)}, bf16[65,256,256]{2,1,0:T(8,128)(2,1)S(1)}, u32[]{:S(2)}) %copy-start) | copy-done | bytes 8519704
  45.4 9.0 %all-to-all-done = bf16[8,128,128]{2,1,0:T(8,128)(2,1)S(1)} async-done(((bf16[8,128,128]{2,1,0:T(8,128)(2,1)}), bf16[8,128,128]{2,1,0:T(8,128)(2,1)S(1)}, u32[]{:S(2)}, u32[]{:S(2)}) %all-to-all-start) | async-done | bytes 262176 | tf_op jit(solution)/shard_map/all_to_all | solution.py:191
  54.4 4.8 %collective-permute-start.3 = (bf16[1024,128]{1,0:T(8,128)(2,1)S(1)}, bf16[1024,128]{1,0:T(8,128)(2,1)S(1)}, u32[]{:S(2)}, u32[]{:S(2)}) collective-permute-start(bf16[1024,128]{1,0:T(8,128)(2,1)S(1)} %bitcast.44), channel_id=1, source_target_pairs={{0,64},{1,9},{2,66},{3,11},{4,68},{5,13},{6,70},{7,15},{8,72},{9,1... | collective-permute-start | bytes 786440 | tf_op jit(solution)/shard_map/ppermute | solution.py:146
  59.2 4.4 %collective-permute-start.5 = (bf16[1024,128]{1,0:T(8,128)(2,1)S(1)}, bf16[1024,128]{1,0:T(8,128)(2,1)S(1)}, u32[]{:S(2)}, u32[]{:S(2)}) collective-permute-start(bf16[1024,128]{1,0:T(8,128)(2,1)S(1)} %bitcast.45), channel_id=1, source_target_pairs={{0,128},{1,17},{2,130},{3,19},{4,132},{5,21},{6,134},{7,23},{8,136... | collective-permute-start | bytes 786440 | tf_op jit(solution)/shard_map/ppermute | solution.py:146
  63.6 4.8 %collective-permute-start.4 = (bf16[1024,128]{1,0:T(8,128)(2,1)S(1)}, bf16[1024,128]{1,0:T(8,128)(2,1)S(1)}, u32[]{:S(2)}, u32[]{:S(2)}) collective-permute-start(bf16[1024,128]{1,0:T(8,128)(2,1)S(1)} %bitcast.46), channel_id=1, source_target_pairs={{0,960},{1,57},{2,962},{3,59},{4,964},{5,61},{6,966},{7,63},{8,968... | collective-permute-start | bytes 786440 | tf_op jit(solution)/shard_map/ppermute | solution.py:146
  68.5 4.3 %collective-permute-start.2 = (bf16[2,33,64,128]{3,2,1,0:T(8,128)(2,1)S(1)}, bf16[2,33,64,128]{3,2,1,0:T(8,128)(2,1)S(1)}, u32[]{:S(2)}, u32[]{:S(2)}) collective-permute-start(bf16[2,33,64,128]{3,2,1,0:T(8,128)(2,1)S(1)} %shard_map.59.high_ref), channel_id=1, source_target_pairs={{0,4},{4,0},{1,5},{5,1},{2,6},{6,2},{3,7},{7,3},{8,12},{12,8},{9,1... | collective-permute-start | bytes 3244040 | tf_op jit(solution)/shard_map/ppermute | solution.py:199
  72.9 1.5 %collective-permute-done.5 = bf16[1024,128]{1,0:T(8,128)(2,1)S(1)} collective-permute-done((bf16[1024,128]{1,0:T(8,128)(2,1)S(1)}, bf16[1024,128]{1,0:T(8,128)(2,1)S(1)}, u32[]{:S(2)}, u32[]{:S(2)}) %collective-permute-start.5) | collective-permute-done | bytes 262176 | tf_op jit(solution)/shard_map/ppermute | solution.py:146
  74.6 0.1 pad_maximum_fusion
  74.7 3.1 %collective-permute-start.9 = (bf16[4096,128]{1,0:T(8,128)(2,1)S(1)}, bf16[4096,128]{1,0:T(8,128)(2,1)S(1)}, u32[]{:S(2)}, u32[]{:S(2)}) collective-permute-start(bf16[4096,128]{1,0:T(8,128)(2,1)S(1)} %get-tuple-element.26.b_ref), channel_id=1, source_target_pairs={{0,8},{1,65},{2,10},{3,67},{4,12},{5,69},{6,14},{7,71},{8,16},{9,7... | collective-permute-start | bytes 3145736 | tf_op jit(solution)/shard_map/ppermute | solution.py:146
  77.8 2.8 %collective-permute-start.8 = (bf16[4096,128]{1,0:T(8,128)(2,1)S(1)}, bf16[4096,128]{1,0:T(8,128)(2,1)S(1)}, u32[]{:S(2)}, u32[]{:S(2)}) collective-permute-start(bf16[4096,128]{1,0:T(8,128)(2,1)S(1)} %get-tuple-element.26.b_ref), channel_id=1, source_target_pairs={{0,56},{1,961},{2,58},{3,963},{4,60},{5,965},{6,62},{7,967},{8,0},... | collective-permute-start | bytes 3145736 | tf_op jit(solution)/shard_map/ppermute | solution.py:146
  80.5 6.4 %collective-permute-start.7 = (bf16[2048,128]{1,0:T(8,128)(2,1)S(1)}, bf16[2048,128]{1,0:T(8,128)(2,1)S(1)}, u32[]{:S(2)}, u32[]{:S(2)}) collective-permute-start(bf16[2048,128]{1,0:T(8,128)(2,1)S(1)} %get-tuple-element.25), channel_id=1, source_target_pairs={{0,16},{1,129},{2,18},{3,131},{4,20},{5,133},{6,22},{7,135},{8,24}... | collective-permute-start | bytes 1572872 | tf_op jit(solution)/shard_map/ppermute | solution.py:146
  87.0 1.9 %collective-permute-start.6 = (bf16[2048,128]{1,0:T(8,128)(2,1)S(1)}, bf16[2048,128]{1,0:T(8,128)(2,1)S(1)}, u32[]{:S(2)}, u32[]{:S(2)}) collective-permute-start(bf16[2048,128]{1,0:T(8,128)(2,1)S(1)} %get-tuple-element.24), channel_id=1, source_target_pairs={{0,48},{1,897},{2,50},{3,899},{4,52},{5,901},{6,54},{7,903},{8,56}... | collective-permute-start | bytes 1572872 | tf_op jit(solution)/shard_map/ppermute | solution.py:146
  88.9 1.3 %collective-permute-done.2.high_ref = bf16[2,33,64,128]{3,2,1,0:T(8,128)(2,1)S(1)} collective-permute-done((bf16[2,33,64,128]{3,2,1,0:T(8,128)(2,1)S(1)}, bf16[2,33,64,128]{3,2,1,0:T(8,128)(2,1)S(1)}, u32[]{:S(2)}, u32[]{:S(2)}) %collective-permute-start.2) | collective-permute-done | bytes 1081376 | tf_op jit(solution)/shard_map/ppermute | solution.py:199
  90.3 6.3 %shard_map.61.other_ref = bf16[65,256,256]{2,1,0:T(8,128)(2,1)S(1)} custom-call(s32[4,64]{1,0:T(4,128)S(1)} %fusion.31.pos_ref, bf16[2,33,64,128]{3,2,1,0:T(8,128)(2,1)S(1)} %collective-permute-done.1.low_ref, bf16[2,33,64,128]{3,2,1,0:T(8,128)(2,1)S(1)} %collective-permute-done.2.high_ref), custom_call_target="tpu_custom_call" | custom-call | bytes 20971520 | tf_op jit(solution)/shard_map/pallas_call | solution.py:81
  96.7 1.5 %shard_map.62.rest_0_ = f32[2,256,128]{2,1,0:T(8,128)S(1)} custom-call(bf16[65,256,256]{2,1,0:T(8,128)(2,1)S(1)} %copy-done.1, bf16[65,256,256]{2,1,0:T(8,128)(2,1)S(1)} %shard_map.61.other_ref, bf16[4096,128]{1,0:T(8,128)(2,1)S(1)} %get-tuple-element.26.b_ref), custom_call_target="tpu_custom_call" | custom-call | flops 536870912 | bytes 4194304 | tf_op jit(solution)/shard_map/pallas_call | solution.py:121
  98.2 1.5 %shard_map.63.rest_0_ = f32[2,256,128]{2,1,0:T(8,128)S(1)} custom-call(bf16[65,256,256]{2,1,0:T(8,128)(2,1)S(1)} %copy-done.1, bf16[65,256,256]{2,1,0:T(8,128)(2,1)S(1)} %shard_map.61.other_ref, bf16[4096,128]{1,0:T(8,128)(2,1)S(1)} %collective-permute-done.9.b_ref, f32[2,256,128]{2,1,0:T(8,128)S(1)} %shard_map.62.rest_0_), custom_call_target="tpu_custom_call" | custom-call | flops 536870912 | bytes 4194304 | tf_op jit(solution)/shard_map/pallas_call | solution.py:121
  99.7 1.5 %shard_map.64.rest_0_ = f32[2,256,128]{2,1,0:T(8,128)S(1)} custom-call(bf16[65,256,256]{2,1,0:T(8,128)(2,1)S(1)} %copy-done.1, bf16[65,256,256]{2,1,0:T(8,128)(2,1)S(1)} %shard_map.61.other_ref, bf16[4096,128]{1,0:T(8,128)(2,1)S(1)} %collective-permute-done.8.b_ref, f32[2,256,128]{2,1,0:T(8,128)S(1)} %shard_map.63.rest_0_), custom_call_target="tpu_custom_call" | custom-call | flops 536870912 | bytes 4194304 | tf_op jit(solution)/shard_map/pallas_call | solution.py:121
  101.2 0.7 shard_map.65.rest_0_
  101.9 7.1 %collective-permute-done.6.b_ref = bf16[2048,128]{1,0:T(8,128)(2,1)S(1)} collective-permute-done((bf16[2048,128]{1,0:T(8,128)(2,1)S(1)}, bf16[2048,128]{1,0:T(8,128)(2,1)S(1)}, u32[]{:S(2)}, u32[]{:S(2)}) %collective-permute-start.6) | collective-permute-done | bytes 524320 | tf_op jit(solution)/shard_map/ppermute | solution.py:146
  109.0 0.7 shard_map.66
  109.8 10.7 %all_to_all.10 = f32[8,64,128]{2,1,0:T(8,128)S(1)} all-to-all(f32[8,64,128]{2,1,0:T(8,128)S(1)} %bitcast.49), channel_id=1, replica_groups=mesh['zf'=4,'zn'=4,'yf'=2,'yn'=4,'xh'=2,'xl'=2,'c'=2] {'xh','xl','c'}, dimensions={0} | all-to-all | bytes 524288 | tf_op jit(solution)/shard_map/all_to_all | solution.py:212
  120.6 0.6 fusion.1
  (30 shorter events, 0.5 us)
Async XLA Ops:
  0.7 8.8 %collective-permute-start = (bf16[64,128]{1,0:T(8,128)(2,1)S(1)}, bf16[64,128]{1,0:T(8,128)(2,1)S(1)}, u32[]{:S(2)}, u32[]{:S(2)}) collective-permute-start(bf16[64,128]{1,0:T(8,128)(2,1)S(1)} %get-tuple-element.44), channel_id=1, source_target_pairs={{0,4},{4,0},{1,5},{5,1},{2,6},{6,2},{3,7},{7,3},{8,12},{12,8},{9,1... | collective-permute-start | bytes 49160 | tf_op jit(solution)/shard_map/ppermute | solution.py:183
  6.5 2.2 %copy-start.2 = (bf16[4,1,64,64,64]{4,3,2,1,0:T(8,128)(2,1)S(1)}, bf16[4,1,64,64,64]{4,3,2,1,0:T(8,128)(2,1)}, u32[]{:S(2)}) copy-start(bf16[4,1,64,64,64]{4,3,2,1,0:T(8,128)(2,1)} %a_ref.3) | copy-start | bytes 6291460
  9.6 54.0 %collective-permute-start.1 = (bf16[2,33,64,128]{3,2,1,0:T(8,128)(2,1)S(1)}, bf16[2,33,64,128]{3,2,1,0:T(8,128)(2,1)S(1)}, u32[]{:S(2)}, u32[]{:S(2)}) collective-permute-start(bf16[2,33,64,128]{3,2,1,0:T(8,128)(2,1)S(1)} %shard_map.58.low_ref), channel_id=1, source_target_pairs={{0,4},{4,0},{1,5},{5,1},{2,6},{6,2},{3,7},{7,3},{8,12},{12,8},{9,1... | collective-permute-start | bytes 3244040 | tf_op jit(solution)/shard_map/ppermute | solution.py:189
  13.6 40.8 %all-to-all-start = ((bf16[8,128,128]{2,1,0:T(8,128)(2,1)}), bf16[8,128,128]{2,1,0:T(8,128)(2,1)S(1)}, u32[]{:S(2)}, u32[]{:S(2)}) async-start(bf16[8,128,128]{2,1,0:T(8,128)(2,1)} %broadcast_in_dim.34), calls=%async_computation | async-start | bytes 524288 | tf_op jit(solution)/shard_map/all_to_all | solution.py:191
  42.1 3.3 %copy-start = (bf16[65,256,256]{2,1,0:T(8,128)(2,1)}, bf16[65,256,256]{2,1,0:T(8,128)(2,1)S(1)}, u32[]{:S(2)}) copy-start(bf16[65,256,256]{2,1,0:T(8,128)(2,1)S(1)} %shard_map.60.own_ref) | copy-start | bytes 25559044
  54.4 18.4 %collective-permute-start.3 = (bf16[1024,128]{1,0:T(8,128)(2,1)S(1)}, bf16[1024,128]{1,0:T(8,128)(2,1)S(1)}, u32[]{:S(2)}, u32[]{:S(2)}) collective-permute-start(bf16[1024,128]{1,0:T(8,128)(2,1)S(1)} %bitcast.44), channel_id=1, source_target_pairs={{0,64},{1,9},{2,66},{3,11},{4,68},{5,13},{6,70},{7,15},{8,72},{9,1... | collective-permute-start | bytes 786440 | tf_op jit(solution)/shard_map/ppermute | solution.py:146
  59.2 15.1 %collective-permute-start.5 = (bf16[1024,128]{1,0:T(8,128)(2,1)S(1)}, bf16[1024,128]{1,0:T(8,128)(2,1)S(1)}, u32[]{:S(2)}, u32[]{:S(2)}) collective-permute-start(bf16[1024,128]{1,0:T(8,128)(2,1)S(1)} %bitcast.45), channel_id=1, source_target_pairs={{0,128},{1,17},{2,130},{3,19},{4,132},{5,21},{6,134},{7,23},{8,136... | collective-permute-start | bytes 786440 | tf_op jit(solution)/shard_map/ppermute | solution.py:146
  63.6 9.2 %collective-permute-start.4 = (bf16[1024,128]{1,0:T(8,128)(2,1)S(1)}, bf16[1024,128]{1,0:T(8,128)(2,1)S(1)}, u32[]{:S(2)}, u32[]{:S(2)}) collective-permute-start(bf16[1024,128]{1,0:T(8,128)(2,1)S(1)} %bitcast.46), channel_id=1, source_target_pairs={{0,960},{1,57},{2,962},{3,59},{4,964},{5,61},{6,966},{7,63},{8,968... | collective-permute-start | bytes 786440 | tf_op jit(solution)/shard_map/ppermute | solution.py:146
  68.5 21.8 %collective-permute-start.2 = (bf16[2,33,64,128]{3,2,1,0:T(8,128)(2,1)S(1)}, bf16[2,33,64,128]{3,2,1,0:T(8,128)(2,1)S(1)}, u32[]{:S(2)}, u32[]{:S(2)}) collective-permute-start(bf16[2,33,64,128]{3,2,1,0:T(8,128)(2,1)S(1)} %shard_map.59.high_ref), channel_id=1, source_target_pairs={{0,4},{4,0},{1,5},{5,1},{2,6},{6,2},{3,7},{7,3},{8,12},{12,8},{9,1... | collective-permute-start | bytes 3244040 | tf_op jit(solution)/shard_map/ppermute | solution.py:199
  74.7 23.5 %collective-permute-start.9 = (bf16[4096,128]{1,0:T(8,128)(2,1)S(1)}, bf16[4096,128]{1,0:T(8,128)(2,1)S(1)}, u32[]{:S(2)}, u32[]{:S(2)}) collective-permute-start(bf16[4096,128]{1,0:T(8,128)(2,1)S(1)} %get-tuple-element.26.b_ref), channel_id=1, source_target_pairs={{0,8},{1,65},{2,10},{3,67},{4,12},{5,69},{6,14},{7,71},{8,16},{9,7... | collective-permute-start | bytes 3145736 | tf_op jit(solution)/shard_map/ppermute | solution.py:146
  77.8 21.9 %collective-permute-start.8 = (bf16[4096,128]{1,0:T(8,128)(2,1)S(1)}, bf16[4096,128]{1,0:T(8,128)(2,1)S(1)}, u32[]{:S(2)}, u32[]{:S(2)}) collective-permute-start(bf16[4096,128]{1,0:T(8,128)(2,1)S(1)} %get-tuple-element.26.b_ref), channel_id=1, source_target_pairs={{0,56},{1,961},{2,58},{3,963},{4,60},{5,965},{6,62},{7,967},{8,0},... | collective-permute-start | bytes 3145736 | tf_op jit(solution)/shard_map/ppermute | solution.py:146
  80.5 20.6 %collective-permute-start.7 = (bf16[2048,128]{1,0:T(8,128)(2,1)S(1)}, bf16[2048,128]{1,0:T(8,128)(2,1)S(1)}, u32[]{:S(2)}, u32[]{:S(2)}) collective-permute-start(bf16[2048,128]{1,0:T(8,128)(2,1)S(1)} %get-tuple-element.25), channel_id=1, source_target_pairs={{0,16},{1,129},{2,18},{3,131},{4,20},{5,133},{6,22},{7,135},{8,24}... | collective-permute-start | bytes 1572872 | tf_op jit(solution)/shard_map/ppermute | solution.py:146
  87.0 22.1 %collective-permute-start.6 = (bf16[2048,128]{1,0:T(8,128)(2,1)S(1)}, bf16[2048,128]{1,0:T(8,128)(2,1)S(1)}, u32[]{:S(2)}, u32[]{:S(2)}) collective-permute-start(bf16[2048,128]{1,0:T(8,128)(2,1)S(1)} %get-tuple-element.24), channel_id=1, source_target_pairs={{0,48},{1,897},{2,50},{3,899},{4,52},{5,901},{6,54},{7,903},{8,56}... | collective-permute-start | bytes 1572872 | tf_op jit(solution)/shard_map/ppermute | solution.py:146
  90.3 6.4 %copy-start.1 = (bf16[65,256,256]{2,1,0:T(8,128)(2,1)S(1)}, bf16[65,256,256]{2,1,0:T(8,128)(2,1)}, u32[]{:S(2)}) copy-start(bf16[65,256,256]{2,1,0:T(8,128)(2,1)} %copy-done) | copy-start | bytes 25559044
  109.8 10.8 %copy-start.3 = (bf16[64,256]{1,0:T(8,128)(2,1)S(1)}, bf16[64,256]{1,0:T(8,128)(2,1)}, u32[]{:S(2)}) copy-start(bf16[64,256]{1,0:T(8,128)(2,1)} %param.5) | copy-start | bytes 98308
